TPU v7x, 512 devices: a whole 4x8x8 slice. The times are simulated.
512 devices in a mesh: mp: 64 (over y, z_hi, core), server: 8 (over x, z_lo).
Axes of the slice: x: 4, y: 8, z: 8 (z_hi: 4, z_lo: 2; z = z_hi * 2 + z_lo), core: 2. Of those that a mesh axis runs over, the one named last changes fastest.
Arguments:
- velocity_start: float32 [2, 4096, 1024], P(None, 'mp', 'server'), may hold values from -6 to 6
- stress_start: float32 [3, 4096, 1024], P(None, 'mp', 'server'), may hold values from -6 to 6
- wind_stress: float32 [2, 4096, 1024], P(None, 'mp', 'server'), may hold values from -6 to 6
- strength: float32 [4096, 1024], P('mp', 'server'), may hold values from 0.5 to 2
- ice_mass: float32 [4096, 1024], P('mp', 'server'), may hold values from 0.5 to 2
- ice_mask: int32 [4096, 1024], P('mp', 'server'), may hold values from 0 to 1, as said below
- send_list: int32 [64, 8, 5, 8], P('mp', 'server'), may hold values from 0 to 63
- block_index: int32 [64, 8, 8, 4], P('mp', 'server'), may hold values from 0 to 39, as said below
- span_slot: int32 [64, 8, 8], P('mp', 'server'), may hold values from 0 to 7, each once within a row
- remap_weights: bfloat16 [64, 8, 8, 4, 128, 128], P('mp', 'server'), may hold values from 0 to 0.00390625
Outputs:
- model_state: float32 [5, 4096, 1024], P(None, 'mp', 'server')
- written: float32 [64, 8, 6, 8, 128], P('mp', 'server')
Inputs may be any that keep to these rules, and one draw needn't show every extreme that they name: `ice_mask`: 1 marks an ice-covered cell. The device d + 2 - block_index // 8 along mp always exists.
All inputs are finite; a program needn't handle non-finite values.
Results may differ from a plain program's by a relative error of at most 0.00075.
Values may be sent and summed in bfloat16 or wider, within the bound.
A program may use at most 64 MiB of HBM per device.

v0:
```python
import jax
import jax.numpy as jnp
from jax import lax
from jax.sharding import PartitionSpec as P

ITERS = 20


RELAXATION = 0.1
STEP_SIZE = 0.3
DRAG_RATE = 1.0
DELTA_MIN = 0.5
ECC_SQUARED = 4.0
FRAC_FLOOR = 0.3


def extended(block, sides, width):
    for axis, dim in sides:
        count = lax.axis_size(axis)
        forward = [(i, i + 1) for i in range(count - 1)]
        backward = [(target, source) for source, target in forward]
        low = lax.ppermute(
            lax.slice_in_dim(block, block.shape[dim] - width, None, axis=dim), axis, forward
        )
        high = lax.ppermute(lax.slice_in_dim(block, 0, width, axis=dim), axis, backward)
        block = jnp.concatenate([low, block, high], axis=dim)
    return block


def from_behind(value, axis, steps):
    count = lax.axis_size(axis)
    leading, last = (max(0, -steps), min(count, count - steps))
    return lax.ppermute(value, axis, [(source, source + steps) for source in range(leading, last)])


def trim_rim(array, amount):
    if amount == 0:
        return array
    return array[..., amount : array.shape[-2] - amount, amount : array.shape[-1] - amount]


def along_x(field):
    return (field[..., 1:-1, 2:] - field[..., 1:-1, :-2]) * 0.5


def along_y(field):
    return (field[..., 2:, 1:-1] - field[..., :-2, 1:-1]) * 0.5


def subcycle(fields, statics):
    statics_now = trim_rim(statics, (statics.shape[-1] - fields.shape[-1]) // 2)
    vel_x, vel_y, sig_one, sig_two, sig_shear = (
        fields[0],
        fields[1],
        fields[2],
        fields[3],
        fields[4],
    )
    divergence = along_x(vel_x) + along_y(vel_y)
    tension = along_x(vel_x) - along_y(vel_y)
    shear_rate = along_y(vel_x) + along_x(vel_y)
    deform = jnp.sqrt(
        divergence * divergence + (tension * tension + shear_rate * shear_rate) / ECC_SQUARED
    )
    ice_load = trim_rim(statics_now[1] * statics_now[0], 1)
    bulk_visc = ice_load / (2.0 * (deform + DELTA_MIN))
    pressure = ice_load * deform / (deform + DELTA_MIN)
    new_one = (trim_rim(sig_one, 1) + RELAXATION * (bulk_visc * divergence - 0.5 * pressure)) / (
        1.0 + RELAXATION
    )
    new_two = (trim_rim(sig_two, 1) + RELAXATION * bulk_visc * tension / ECC_SQUARED) / (
        1.0 + RELAXATION
    )
    new_shear = (trim_rim(sig_shear, 1) + RELAXATION * bulk_visc * shear_rate / ECC_SQUARED) / (
        1.0 + RELAXATION
    )
    force_x = along_x(0.5 * (new_one + new_two)) + along_y(new_shear)
    force_y = along_x(new_shear) + along_y(0.5 * (new_one - new_two))
    interior = trim_rim(statics_now, 2)
    covered = interior[0] > 0.5
    next_x = jnp.where(
        covered,
        (trim_rim(vel_x, 2) + STEP_SIZE * (force_x + interior[3]) / interior[2])
        / (1.0 + STEP_SIZE * DRAG_RATE),
        0.0,
    )
    next_y = jnp.where(
        covered,
        (trim_rim(vel_y, 2) + STEP_SIZE * (force_y + interior[4]) / interior[2])
        / (1.0 + STEP_SIZE * DRAG_RATE),
        0.0,
    )
    stacked = jnp.stack(
        [next_x, next_y, trim_rim(new_one, 1), trim_rim(new_two, 1), trim_rim(new_shear, 1)]
    )
    return (stacked, trim_rim(pressure, 1))


def body(
    velocity_start,
    stress_start,
    wind_stress,
    strength,
    ice_mass,
    ice_mask,
    send_list,
    block_index,
    span_slot,
    remap_weights,
):
    repeat = 1
    rim_width = 2 * repeat
    ice_float = ice_mask.astype(jnp.float32)
    statics = jnp.stack([ice_float, strength, ice_mass, wind_stress[0], wind_stress[1]])
    statics = extended(statics, (("mp", 1), ("server", 2)), rim_width)
    fields = jnp.concatenate([velocity_start, stress_start], axis=0)
    pressure = jnp.zeros(ice_float.shape, jnp.float32)

    def advance(step_index, state_pair):
        current, last_pressure = state_pair
        padded = extended(current, (("mp", 1), ("server", 2)), rim_width)
        padded, last_pressure = subcycle(padded, statics)
        return (padded, last_pressure)

    fields, pressure = lax.fori_loop(0, ITERS // repeat, advance, (fields, pressure))
    field_rows = jnp.concatenate([fields, pressure[None], ice_float[None]], axis=0).astype(
        jnp.bfloat16
    )
    offset_count = send_list.shape[2]
    slot_count = send_list.shape[3]
    reach_now = (offset_count - 1) // 2
    row_width = field_rows.shape[2]
    outgoing = jnp.take(field_rows, send_list.reshape(-1), axis=1).reshape(
        7, offset_count, slot_count, row_width
    )
    pieces = []
    for offset in range(offset_count):
        shift_by = offset - reach_now
        if shift_by == 0:
            pieces.append(outgoing[:, offset])
        else:
            pieces.append(from_behind(outgoing[:, offset], "mp", shift_by))
    incoming = jnp.stack(pieces, axis=1)
    received = incoming.reshape(7, offset_count * slot_count, row_width)
    weights = remap_weights[0, 0]
    block_total = weights.shape[0]
    intersection_count = weights.shape[1]
    blocks = jnp.take(received, block_index.reshape(-1), axis=1).reshape(
        7, block_total, intersection_count, row_width
    )
    totals = jnp.einsum("frkc,rkcq->frq", blocks, weights, preferred_element_type=jnp.float32)
    remapped = totals[:6] / jnp.maximum(totals[6:7], FRAC_FLOOR)
    inverse = jnp.argsort(span_slot[0, 0])
    ordered = jnp.take(remapped, inverse, axis=1)
    written = lax.all_to_all(ordered[None, None], "server", split_axis=3, concat_axis=3, tiled=True)
    return (fields, written)


def solution(mesh):
    placed = (
        P(None, "mp", "server"),
        P(None, "mp", "server"),
        P(None, "mp", "server"),
        P("mp", "server"),
        P("mp", "server"),
        P("mp", "server"),
        P("mp", "server", None, None),
        P("mp", "server", None, None),
        P("mp", "server", None),
        P("mp", "server", None, None, None, None),
    )
    return jax.shard_map(
        body,
        mesh=mesh,
        in_specs=placed,
        out_specs=(P(None, "mp", "server"), P("mp", "server", None, None, None)),
        check_vma=False,
    )
```

profile of v0, /device:TPU:33, one launch (start us, length us, event | category | flops | bytes accessed | tf_op | source)
XLA Modules:
  0.0 536.5 jit_solution(7713478769839239771)
XLA Ops:
  2.3 6.5 %collective-permute-start.4 = (f32[5,2,128]{2,1,0:T(2,128)S(1)}, f32[5,2,128]{2,1,0:T(2,128)S(1)}, u32[]{:S(2)}, u32[]{:S(2)}) collective-permute-start(f32[5,2,128]{2,1,0:T(2,128)S(1)} %get-tuple-element.145), channel_id=1, source_target_pairs={{0,8},{8,16},{16,24},{24,32},{32,40},{40,48},{48,56},{56,64},{64,7... | collective-permute-start | bytes 15368 | tf_op jit(solution)/shard_map/ppermute | solution.py:22
  15.0 4.0 collective-permute-start.6
  21.4 5.7 %collective-permute-done.7 = f32[5,68,2]{2,1,0:T(8,128)S(1)} collective-permute-done((f32[5,68,2]{2,1,0:T(8,128)S(1)}, f32[5,68,2]{2,1,0:T(8,128)S(1)}, u32[]{:S(2)}, u32[]{:S(2)}) %collective-permute-start.7) | collective-permute-done | bytes 2752 | tf_op jit(solution)/shard_map/ppermute | solution.py:25
  27.4 465.7 %while.14 = (s32[]{:T(128)}, f32[5,64,128]{2,1,0:T(8,128)S(1)}, bf16[64,128]{1,0:T(8,128)(2,1)}, f32[64,128]{1,0:T(8,128)S(1)}, f32[68,132]{1,0:T(8,128)S(1)}, /...) while((s32[]{:T(128)}, f32[5,64,128]{2,1,0:T(8,128)S(1)}, ...), condition=%wide.region_1.2_spmd, body=%wide.region_0.1_spmd.sunk | while | flops 824693 | bytes 2804229 | solution.py:125
  27.4 4.7 collective-permute-start
  34.1 5.3 collective-permute-done.1
  49.1 9.7 %collective-permute-start = (f32[5,2,128]{2,1,0:T(2,128)S(1)}, f32[5,2,128]{2,1,0:T(2,128)S(1)}, u32[]{:S(2)}, u32[]{:S(2)}) collective-permute-start(f32[5,2,128]{2,1,0:T(2,128)S(1)} %get-tuple-element.230), channel_id=1, source_target_pairs={{8,0},{16,8},{24,16},{32,24},{40,32},{48,40},{56,48},{64,56},{72,6... | collective-permute-start | bytes 15368 | tf_op jit(solution)/shard_map/while/body/eval_jaxpr/ppermute | solution.py:25
  63.3 4.7 collective-permute-start.3
  72.3 8.9 %collective-permute-start = (f32[5,2,128]{2,1,0:T(2,128)S(1)}, f32[5,2,128]{2,1,0:T(2,128)S(1)}, u32[]{:S(2)}, u32[]{:S(2)}) collective-permute-start(f32[5,2,128]{2,1,0:T(2,128)S(1)} %get-tuple-element.230), channel_id=1, source_target_pairs={{8,0},{16,8},{24,16},{32,24},{40,32},{48,40},{56,48},{64,56},{72,6... | collective-permute-start | bytes 15368 | tf_op jit(solution)/shard_map/while/body/eval_jaxpr/ppermute | solution.py:25
  85.7 5.7 %collective-permute-start.3 = (f32[5,68,2]{2,1,0:T(8,128)S(1)}, f32[5,68,2]{2,1,0:T(8,128)S(1)}, u32[]{:S(2)}, u32[]{:S(2)}) collective-permute-start(f32[5,68,2]{2,1,0:T(8,128)S(1)} %get-tuple-element.233), channel_id=1, source_target_pairs={{0,1},{1,2},{2,3},{3,4},{4,5},{5,6},{6,7},{8,9},{9,10},{10,11},{11... | collective-permute-start | bytes 8168 | tf_op jit(solution)/shard_map/while/body/eval_jaxpr/ppermute | solution.py:22
  95.6 8.9 %collective-permute-start = (f32[5,2,128]{2,1,0:T(2,128)S(1)}, f32[5,2,128]{2,1,0:T(2,128)S(1)}, u32[]{:S(2)}, u32[]{:S(2)}) collective-permute-start(f32[5,2,128]{2,1,0:T(2,128)S(1)} %get-tuple-element.230), channel_id=1, source_target_pairs={{8,0},{16,8},{24,16},{32,24},{40,32},{48,40},{56,48},{64,56},{72,6... | collective-permute-start | bytes 15368 | tf_op jit(solution)/shard_map/while/body/eval_jaxpr/ppermute | solution.py:25
  109.0 5.8 %collective-permute-start.3 = (f32[5,68,2]{2,1,0:T(8,128)S(1)}, f32[5,68,2]{2,1,0:T(8,128)S(1)}, u32[]{:S(2)}, u32[]{:S(2)}) collective-permute-start(f32[5,68,2]{2,1,0:T(8,128)S(1)} %get-tuple-element.233), channel_id=1, source_target_pairs={{0,1},{1,2},{2,3},{3,4},{4,5},{5,6},{6,7},{8,9},{9,10},{10,11},{11... | collective-permute-start | bytes 8168 | tf_op jit(solution)/shard_map/while/body/eval_jaxpr/ppermute | solution.py:22
  119.1 8.9 %collective-permute-start = (f32[5,2,128]{2,1,0:T(2,128)S(1)}, f32[5,2,128]{2,1,0:T(2,128)S(1)}, u32[]{:S(2)}, u32[]{:S(2)}) collective-permute-start(f32[5,2,128]{2,1,0:T(2,128)S(1)} %get-tuple-element.230), channel_id=1, source_target_pairs={{8,0},{16,8},{24,16},{32,24},{40,32},{48,40},{56,48},{64,56},{72,6... | collective-permute-start | bytes 15368 | tf_op jit(solution)/shard_map/while/body/eval_jaxpr/ppermute | solution.py:25
  132.4 5.8 %collective-permute-start.3 = (f32[5,68,2]{2,1,0:T(8,128)S(1)}, f32[5,68,2]{2,1,0:T(8,128)S(1)}, u32[]{:S(2)}, u32[]{:S(2)}) collective-permute-start(f32[5,68,2]{2,1,0:T(8,128)S(1)} %get-tuple-element.233), channel_id=1, source_target_pairs={{0,1},{1,2},{2,3},{3,4},{4,5},{5,6},{6,7},{8,9},{9,10},{10,11},{11... | collective-permute-start | bytes 8168 | tf_op jit(solution)/shard_map/while/body/eval_jaxpr/ppermute | solution.py:22
  142.5 8.9 %collective-permute-start = (f32[5,2,128]{2,1,0:T(2,128)S(1)}, f32[5,2,128]{2,1,0:T(2,128)S(1)}, u32[]{:S(2)}, u32[]{:S(2)}) collective-permute-start(f32[5,2,128]{2,1,0:T(2,128)S(1)} %get-tuple-element.230), channel_id=1, source_target_pairs={{8,0},{16,8},{24,16},{32,24},{40,32},{48,40},{56,48},{64,56},{72,6... | collective-permute-start | bytes 15368 | tf_op jit(solution)/shard_map/while/body/eval_jaxpr/ppermute | solution.py:25
  155.9 5.9 %collective-permute-start.3 = (f32[5,68,2]{2,1,0:T(8,128)S(1)}, f32[5,68,2]{2,1,0:T(8,128)S(1)}, u32[]{:S(2)}, u32[]{:S(2)}) collective-permute-start(f32[5,68,2]{2,1,0:T(8,128)S(1)} %get-tuple-element.233), channel_id=1, source_target_pairs={{0,1},{1,2},{2,3},{3,4},{4,5},{5,6},{6,7},{8,9},{9,10},{10,11},{11... | collective-permute-start | bytes 8168 | tf_op jit(solution)/shard_map/while/body/eval_jaxpr/ppermute | solution.py:22
  166.0 8.9 %collective-permute-start = (f32[5,2,128]{2,1,0:T(2,128)S(1)}, f32[5,2,128]{2,1,0:T(2,128)S(1)}, u32[]{:S(2)}, u32[]{:S(2)}) collective-permute-start(f32[5,2,128]{2,1,0:T(2,128)S(1)} %get-tuple-element.230), channel_id=1, source_target_pairs={{8,0},{16,8},{24,16},{32,24},{40,32},{48,40},{56,48},{64,56},{72,6... | collective-permute-start | bytes 15368 | tf_op jit(solution)/shard_map/while/body/eval_jaxpr/ppermute | solution.py:25
  179.4 5.8 %collective-permute-start.3 = (f32[5,68,2]{2,1,0:T(8,128)S(1)}, f32[5,68,2]{2,1,0:T(8,128)S(1)}, u32[]{:S(2)}, u32[]{:S(2)}) collective-permute-start(f32[5,68,2]{2,1,0:T(8,128)S(1)} %get-tuple-element.233), channel_id=1, source_target_pairs={{0,1},{1,2},{2,3},{3,4},{4,5},{5,6},{6,7},{8,9},{9,10},{10,11},{11... | collective-permute-start | bytes 8168 | tf_op jit(solution)/shard_map/while/body/eval_jaxpr/ppermute | solution.py:22
  189.5 8.9 %collective-permute-start = (f32[5,2,128]{2,1,0:T(2,128)S(1)}, f32[5,2,128]{2,1,0:T(2,128)S(1)}, u32[]{:S(2)}, u32[]{:S(2)}) collective-permute-start(f32[5,2,128]{2,1,0:T(2,128)S(1)} %get-tuple-element.230), channel_id=1, source_target_pairs={{8,0},{16,8},{24,16},{32,24},{40,32},{48,40},{56,48},{64,56},{72,6... | collective-permute-start | bytes 15368 | tf_op jit(solution)/shard_map/while/body/eval_jaxpr/ppermute | solution.py:25
  202.9 5.8 %collective-permute-start.3 = (f32[5,68,2]{2,1,0:T(8,128)S(1)}, f32[5,68,2]{2,1,0:T(8,128)S(1)}, u32[]{:S(2)}, u32[]{:S(2)}) collective-permute-start(f32[5,68,2]{2,1,0:T(8,128)S(1)} %get-tuple-element.233), channel_id=1, source_target_pairs={{0,1},{1,2},{2,3},{3,4},{4,5},{5,6},{6,7},{8,9},{9,10},{10,11},{11... | collective-permute-start | bytes 8168 | tf_op jit(solution)/shard_map/while/body/eval_jaxpr/ppermute | solution.py:22
  212.9 8.9 %collective-permute-start = (f32[5,2,128]{2,1,0:T(2,128)S(1)}, f32[5,2,128]{2,1,0:T(2,128)S(1)}, u32[]{:S(2)}, u32[]{:S(2)}) collective-permute-start(f32[5,2,128]{2,1,0:T(2,128)S(1)} %get-tuple-element.230), channel_id=1, source_target_pairs={{8,0},{16,8},{24,16},{32,24},{40,32},{48,40},{56,48},{64,56},{72,6... | collective-permute-start | bytes 15368 | tf_op jit(solution)/shard_map/while/body/eval_jaxpr/ppermute | solution.py:25
  226.3 5.8 %collective-permute-start.3 = (f32[5,68,2]{2,1,0:T(8,128)S(1)}, f32[5,68,2]{2,1,0:T(8,128)S(1)}, u32[]{:S(2)}, u32[]{:S(2)}) collective-permute-start(f32[5,68,2]{2,1,0:T(8,128)S(1)} %get-tuple-element.233), channel_id=1, source_target_pairs={{0,1},{1,2},{2,3},{3,4},{4,5},{5,6},{6,7},{8,9},{9,10},{10,11},{11... | collective-permute-start | bytes 8168 | tf_op jit(solution)/shard_map/while/body/eval_jaxpr/ppermute | solution.py:22
  236.4 8.9 %collective-permute-start = (f32[5,2,128]{2,1,0:T(2,128)S(1)}, f32[5,2,128]{2,1,0:T(2,128)S(1)}, u32[]{:S(2)}, u32[]{:S(2)}) collective-permute-start(f32[5,2,128]{2,1,0:T(2,128)S(1)} %get-tuple-element.230), channel_id=1, source_target_pairs={{8,0},{16,8},{24,16},{32,24},{40,32},{48,40},{56,48},{64,56},{72,6... | collective-permute-start | bytes 15368 | tf_op jit(solution)/shard_map/while/body/eval_jaxpr/ppermute | solution.py:25
  249.7 5.7 %collective-permute-start.3 = (f32[5,68,2]{2,1,0:T(8,128)S(1)}, f32[5,68,2]{2,1,0:T(8,128)S(1)}, u32[]{:S(2)}, u32[]{:S(2)}) collective-permute-start(f32[5,68,2]{2,1,0:T(8,128)S(1)} %get-tuple-element.233), channel_id=1, source_target_pairs={{0,1},{1,2},{2,3},{3,4},{4,5},{5,6},{6,7},{8,9},{9,10},{10,11},{11... | collective-permute-start | bytes 8168 | tf_op jit(solution)/shard_map/while/body/eval_jaxpr/ppermute | solution.py:22
  259.7 8.9 %collective-permute-start = (f32[5,2,128]{2,1,0:T(2,128)S(1)}, f32[5,2,128]{2,1,0:T(2,128)S(1)}, u32[]{:S(2)}, u32[]{:S(2)}) collective-permute-start(f32[5,2,128]{2,1,0:T(2,128)S(1)} %get-tuple-element.230), channel_id=1, source_target_pairs={{8,0},{16,8},{24,16},{32,24},{40,32},{48,40},{56,48},{64,56},{72,6... | collective-permute-start | bytes 15368 | tf_op jit(solution)/shard_map/while/body/eval_jaxpr/ppermute | solution.py:25
  273.1 5.7 %collective-permute-start.3 = (f32[5,68,2]{2,1,0:T(8,128)S(1)}, f32[5,68,2]{2,1,0:T(8,128)S(1)}, u32[]{:S(2)}, u32[]{:S(2)}) collective-permute-start(f32[5,68,2]{2,1,0:T(8,128)S(1)} %get-tuple-element.233), channel_id=1, source_target_pairs={{0,1},{1,2},{2,3},{3,4},{4,5},{5,6},{6,7},{8,9},{9,10},{10,11},{11... | collective-permute-start | bytes 8168 | tf_op jit(solution)/shard_map/while/body/eval_jaxpr/ppermute | solution.py:22
  283.0 8.9 %collective-permute-start = (f32[5,2,128]{2,1,0:T(2,128)S(1)}, f32[5,2,128]{2,1,0:T(2,128)S(1)}, u32[]{:S(2)}, u32[]{:S(2)}) collective-permute-start(f32[5,2,128]{2,1,0:T(2,128)S(1)} %get-tuple-element.230), channel_id=1, source_target_pairs={{8,0},{16,8},{24,16},{32,24},{40,32},{48,40},{56,48},{64,56},{72,6... | collective-permute-start | bytes 15368 | tf_op jit(solution)/shard_map/while/body/eval_jaxpr/ppermute | solution.py:25
  296.4 5.7 %collective-permute-start.3 = (f32[5,68,2]{2,1,0:T(8,128)S(1)}, f32[5,68,2]{2,1,0:T(8,128)S(1)}, u32[]{:S(2)}, u32[]{:S(2)}) collective-permute-start(f32[5,68,2]{2,1,0:T(8,128)S(1)} %get-tuple-element.233), channel_id=1, source_target_pairs={{0,1},{1,2},{2,3},{3,4},{4,5},{5,6},{6,7},{8,9},{9,10},{10,11},{11... | collective-permute-start | bytes 8168 | tf_op jit(solution)/shard_map/while/body/eval_jaxpr/ppermute | solution.py:22
  306.4 8.9 %collective-permute-start = (f32[5,2,128]{2,1,0:T(2,128)S(1)}, f32[5,2,128]{2,1,0:T(2,128)S(1)}, u32[]{:S(2)}, u32[]{:S(2)}) collective-permute-start(f32[5,2,128]{2,1,0:T(2,128)S(1)} %get-tuple-element.230), channel_id=1, source_target_pairs={{8,0},{16,8},{24,16},{32,24},{40,32},{48,40},{56,48},{64,56},{72,6... | collective-permute-start | bytes 15368 | tf_op jit(solution)/shard_map/while/body/eval_jaxpr/ppermute | solution.py:25
  319.7 5.7 %collective-permute-start.3 = (f32[5,68,2]{2,1,0:T(8,128)S(1)}, f32[5,68,2]{2,1,0:T(8,128)S(1)}, u32[]{:S(2)}, u32[]{:S(2)}) collective-permute-start(f32[5,68,2]{2,1,0:T(8,128)S(1)} %get-tuple-element.233), channel_id=1, source_target_pairs={{0,1},{1,2},{2,3},{3,4},{4,5},{5,6},{6,7},{8,9},{9,10},{10,11},{11... | collective-permute-start | bytes 8168 | tf_op jit(solution)/shard_map/while/body/eval_jaxpr/ppermute | solution.py:22
  329.7 8.9 %collective-permute-start = (f32[5,2,128]{2,1,0:T(2,128)S(1)}, f32[5,2,128]{2,1,0:T(2,128)S(1)}, u32[]{:S(2)}, u32[]{:S(2)}) collective-permute-start(f32[5,2,128]{2,1,0:T(2,128)S(1)} %get-tuple-element.230), channel_id=1, source_target_pairs={{8,0},{16,8},{24,16},{32,24},{40,32},{48,40},{56,48},{64,56},{72,6... | collective-permute-start | bytes 15368 | tf_op jit(solution)/shard_map/while/body/eval_jaxpr/ppermute | solution.py:25
  343.1 5.7 %collective-permute-start.3 = (f32[5,68,2]{2,1,0:T(8,128)S(1)}, f32[5,68,2]{2,1,0:T(8,128)S(1)}, u32[]{:S(2)}, u32[]{:S(2)}) collective-permute-start(f32[5,68,2]{2,1,0:T(8,128)S(1)} %get-tuple-element.233), channel_id=1, source_target_pairs={{0,1},{1,2},{2,3},{3,4},{4,5},{5,6},{6,7},{8,9},{9,10},{10,11},{11... | collective-permute-start | bytes 8168 | tf_op jit(solution)/shard_map/while/body/eval_jaxpr/ppermute | solution.py:22
  353.0 8.9 %collective-permute-start = (f32[5,2,128]{2,1,0:T(2,128)S(1)}, f32[5,2,128]{2,1,0:T(2,128)S(1)}, u32[]{:S(2)}, u32[]{:S(2)}) collective-permute-start(f32[5,2,128]{2,1,0:T(2,128)S(1)} %get-tuple-element.230), channel_id=1, source_target_pairs={{8,0},{16,8},{24,16},{32,24},{40,32},{48,40},{56,48},{64,56},{72,6... | collective-permute-start | bytes 15368 | tf_op jit(solution)/shard_map/while/body/eval_jaxpr/ppermute | solution.py:25
  366.4 5.7 %collective-permute-start.3 = (f32[5,68,2]{2,1,0:T(8,128)S(1)}, f32[5,68,2]{2,1,0:T(8,128)S(1)}, u32[]{:S(2)}, u32[]{:S(2)}) collective-permute-start(f32[5,68,2]{2,1,0:T(8,128)S(1)} %get-tuple-element.233), channel_id=1, source_target_pairs={{0,1},{1,2},{2,3},{3,4},{4,5},{5,6},{6,7},{8,9},{9,10},{10,11},{11... | collective-permute-start | bytes 8168 | tf_op jit(solution)/shard_map/while/body/eval_jaxpr/ppermute | solution.py:22
  376.4 8.9 %collective-permute-start = (f32[5,2,128]{2,1,0:T(2,128)S(1)}, f32[5,2,128]{2,1,0:T(2,128)S(1)}, u32[]{:S(2)}, u32[]{:S(2)}) collective-permute-start(f32[5,2,128]{2,1,0:T(2,128)S(1)} %get-tuple-element.230), channel_id=1, source_target_pairs={{8,0},{16,8},{24,16},{32,24},{40,32},{48,40},{56,48},{64,56},{72,6... | collective-permute-start | bytes 15368 | tf_op jit(solution)/shard_map/while/body/eval_jaxpr/ppermute | solution.py:25
  389.7 5.7 %collective-permute-start.3 = (f32[5,68,2]{2,1,0:T(8,128)S(1)}, f32[5,68,2]{2,1,0:T(8,128)S(1)}, u32[]{:S(2)}, u32[]{:S(2)}) collective-permute-start(f32[5,68,2]{2,1,0:T(8,128)S(1)} %get-tuple-element.233), channel_id=1, source_target_pairs={{0,1},{1,2},{2,3},{3,4},{4,5},{5,6},{6,7},{8,9},{9,10},{10,11},{11... | collective-permute-start | bytes 8168 | tf_op jit(solution)/shard_map/while/body/eval_jaxpr/ppermute | solution.py:22
  399.7 8.9 %collective-permute-start = (f32[5,2,128]{2,1,0:T(2,128)S(1)}, f32[5,2,128]{2,1,0:T(2,128)S(1)}, u32[]{:S(2)}, u32[]{:S(2)}) collective-permute-start(f32[5,2,128]{2,1,0:T(2,128)S(1)} %get-tuple-element.230), channel_id=1, source_target_pairs={{8,0},{16,8},{24,16},{32,24},{40,32},{48,40},{56,48},{64,56},{72,6... | collective-permute-start | bytes 15368 | tf_op jit(solution)/shard_map/while/body/eval_jaxpr/ppermute | solution.py:25
  413.1 5.7 %collective-permute-start.3 = (f32[5,68,2]{2,1,0:T(8,128)S(1)}, f32[5,68,2]{2,1,0:T(8,128)S(1)}, u32[]{:S(2)}, u32[]{:S(2)}) collective-permute-start(f32[5,68,2]{2,1,0:T(8,128)S(1)} %get-tuple-element.233), channel_id=1, source_target_pairs={{0,1},{1,2},{2,3},{3,4},{4,5},{5,6},{6,7},{8,9},{9,10},{10,11},{11... | collective-permute-start | bytes 8168 | tf_op jit(solution)/shard_map/while/body/eval_jaxpr/ppermute | solution.py:22
  423.1 8.9 %collective-permute-start = (f32[5,2,128]{2,1,0:T(2,128)S(1)}, f32[5,2,128]{2,1,0:T(2,128)S(1)}, u32[]{:S(2)}, u32[]{:S(2)}) collective-permute-start(f32[5,2,128]{2,1,0:T(2,128)S(1)} %get-tuple-element.230), channel_id=1, source_target_pairs={{8,0},{16,8},{24,16},{32,24},{40,32},{48,40},{56,48},{64,56},{72,6... | collective-permute-start | bytes 15368 | tf_op jit(solution)/shard_map/while/body/eval_jaxpr/ppermute | solution.py:25
  436.4 5.7 %collective-permute-start.3 = (f32[5,68,2]{2,1,0:T(8,128)S(1)}, f32[5,68,2]{2,1,0:T(8,128)S(1)}, u32[]{:S(2)}, u32[]{:S(2)}) collective-permute-start(f32[5,68,2]{2,1,0:T(8,128)S(1)} %get-tuple-element.233), channel_id=1, source_target_pairs={{0,1},{1,2},{2,3},{3,4},{4,5},{5,6},{6,7},{8,9},{9,10},{10,11},{11... | collective-permute-start | bytes 8168 | tf_op jit(solution)/shard_map/while/body/eval_jaxpr/ppermute | solution.py:22
  446.4 8.9 %collective-permute-start = (f32[5,2,128]{2,1,0:T(2,128)S(1)}, f32[5,2,128]{2,1,0:T(2,128)S(1)}, u32[]{:S(2)}, u32[]{:S(2)}) collective-permute-start(f32[5,2,128]{2,1,0:T(2,128)S(1)} %get-tuple-element.230), channel_id=1, source_target_pairs={{8,0},{16,8},{24,16},{32,24},{40,32},{48,40},{56,48},{64,56},{72,6... | collective-permute-start | bytes 15368 | tf_op jit(solution)/shard_map/while/body/eval_jaxpr/ppermute | solution.py:25
  459.8 5.7 %collective-permute-start.3 = (f32[5,68,2]{2,1,0:T(8,128)S(1)}, f32[5,68,2]{2,1,0:T(8,128)S(1)}, u32[]{:S(2)}, u32[]{:S(2)}) collective-permute-start(f32[5,68,2]{2,1,0:T(8,128)S(1)} %get-tuple-element.233), channel_id=1, source_target_pairs={{0,1},{1,2},{2,3},{3,4},{4,5},{5,6},{6,7},{8,9},{9,10},{10,11},{11... | collective-permute-start | bytes 8168 | tf_op jit(solution)/shard_map/while/body/eval_jaxpr/ppermute | solution.py:22
  469.7 8.9 %collective-permute-start = (f32[5,2,128]{2,1,0:T(2,128)S(1)}, f32[5,2,128]{2,1,0:T(2,128)S(1)}, u32[]{:S(2)}, u32[]{:S(2)}) collective-permute-start(f32[5,2,128]{2,1,0:T(2,128)S(1)} %get-tuple-element.230), channel_id=1, source_target_pairs={{8,0},{16,8},{24,16},{32,24},{40,32},{48,40},{56,48},{64,56},{72,6... | collective-permute-start | bytes 15368 | tf_op jit(solution)/shard_map/while/body/eval_jaxpr/ppermute | solution.py:25
  483.1 5.7 %collective-permute-start.3 = (f32[5,68,2]{2,1,0:T(8,128)S(1)}, f32[5,68,2]{2,1,0:T(8,128)S(1)}, u32[]{:S(2)}, u32[]{:S(2)}) collective-permute-start(f32[5,68,2]{2,1,0:T(8,128)S(1)} %get-tuple-element.233), channel_id=1, source_target_pairs={{0,1},{1,2},{2,3},{3,4},{4,5},{5,6},{6,7},{8,9},{9,10},{10,11},{11... | collective-permute-start | bytes 8168 | tf_op jit(solution)/shard_map/while/body/eval_jaxpr/ppermute | solution.py:22
  494.6 7.1 %collective-permute-start.8 = (bf16[7,8,128]{2,1,0:T(8,128)(2,1)S(1)}, bf16[7,8,128]{2,1,0:T(8,128)(2,1)S(1)}, u32[]{:S(2)}, u32[]{:S(2)}) collective-permute-start(bf16[7,8,128]{2,1,0:T(8,128)(2,1)S(1)} %get-tuple-element.150), channel_id=1, source_target_pairs={{16,0},{24,8},{32,16},{40,24},{48,32},{56,40},{64,48},{72,56},{80,... | collective-permute-start | bytes 43016 | tf_op jit(solution)/shard_map/ppermute | solution.py:33
  505.5 4.4 collective-permute-start.10
  512.1 6.6 %collective-permute-done.11 = bf16[7,8,128]{2,1,0:T(8,128)(2,1)S(1)} collective-permute-done((bf16[7,8,128]{2,1,0:T(8,128)(2,1)S(1)}, bf16[7,8,128]{2,1,0:T(8,128)(2,1)S(1)}, u32[]{:S(2)}, u32[]{:S(2)}) %collective-permute-start.11) | collective-permute-done | bytes 14368 | tf_op jit(solution)/shard_map/ppermute | solution.py:33
  520.3 15.6 %all_to_all.5 = f32[1,1,6,8,128]{4,1,2,0,3:T(1,128)S(1)} all-to-all(f32[1,1,6,8,128]{4,1,2,0,3:T(1,128)S(1)} %copy.64), channel_id=1, replica_groups=mesh['mp'=64,'server'=8] {'server'}, dimensions={3} | all-to-all | bytes 49152 | tf_op jit(solution)/shard_map/all_to_all | solution.py:155
  (456 shorter events, 196.5 us)
Async XLA Ops:
  2.3 9.9 %collective-permute-start.4 = (f32[5,2,128]{2,1,0:T(2,128)S(1)}, f32[5,2,128]{2,1,0:T(2,128)S(1)}, u32[]{:S(2)}, u32[]{:S(2)}) collective-permute-start(f32[5,2,128]{2,1,0:T(2,128)S(1)} %get-tuple-element.145), channel_id=1, source_target_pairs={{0,8},{8,16},{16,24},{24,32},{32,40},{40,48},{48,56},{56,64},{64,7... | collective-permute-start | bytes 15368 | tf_op jit(solution)/shard_map/ppermute | solution.py:22
  19.0 8.1 %collective-permute-start.7 = (f32[5,68,2]{2,1,0:T(8,128)S(1)}, f32[5,68,2]{2,1,0:T(8,128)S(1)}, u32[]{:S(2)}, u32[]{:S(2)}) collective-permute-start(f32[5,68,2]{2,1,0:T(8,128)S(1)} %get-tuple-element.144), channel_id=1, source_target_pairs={{1,0},{2,1},{3,2},{4,3},{5,4},{6,5},{7,6},{9,8},{10,9},{11,10},{12... | collective-permute-start | bytes 8168 | tf_op jit(solution)/shard_map/ppermute | solution.py:25
  49.1 11.6 %collective-permute-start = (f32[5,2,128]{2,1,0:T(2,128)S(1)}, f32[5,2,128]{2,1,0:T(2,128)S(1)}, u32[]{:S(2)}, u32[]{:S(2)}) collective-permute-start(f32[5,2,128]{2,1,0:T(2,128)S(1)} %get-tuple-element.230), channel_id=1, source_target_pairs={{8,0},{16,8},{24,16},{32,24},{40,32},{48,40},{56,48},{64,56},{72,6... | collective-permute-start | bytes 15368 | tf_op jit(solution)/shard_map/while/body/eval_jaxpr/ppermute | solution.py:25
  72.3 10.8 %collective-permute-start = (f32[5,2,128]{2,1,0:T(2,128)S(1)}, f32[5,2,128]{2,1,0:T(2,128)S(1)}, u32[]{:S(2)}, u32[]{:S(2)}) collective-permute-start(f32[5,2,128]{2,1,0:T(2,128)S(1)} %get-tuple-element.230), channel_id=1, source_target_pairs={{8,0},{16,8},{24,16},{32,24},{40,32},{48,40},{56,48},{64,56},{72,6... | collective-permute-start | bytes 15368 | tf_op jit(solution)/shard_map/while/body/eval_jaxpr/ppermute | solution.py:25
  85.7 8.2 %collective-permute-start.3 = (f32[5,68,2]{2,1,0:T(8,128)S(1)}, f32[5,68,2]{2,1,0:T(8,128)S(1)}, u32[]{:S(2)}, u32[]{:S(2)}) collective-permute-start(f32[5,68,2]{2,1,0:T(8,128)S(1)} %get-tuple-element.233), channel_id=1, source_target_pairs={{0,1},{1,2},{2,3},{3,4},{4,5},{5,6},{6,7},{8,9},{9,10},{10,11},{11... | collective-permute-start | bytes 8168 | tf_op jit(solution)/shard_map/while/body/eval_jaxpr/ppermute | solution.py:22
  95.6 10.8 %collective-permute-start = (f32[5,2,128]{2,1,0:T(2,128)S(1)}, f32[5,2,128]{2,1,0:T(2,128)S(1)}, u32[]{:S(2)}, u32[]{:S(2)}) collective-permute-start(f32[5,2,128]{2,1,0:T(2,128)S(1)} %get-tuple-element.230), channel_id=1, source_target_pairs={{8,0},{16,8},{24,16},{32,24},{40,32},{48,40},{56,48},{64,56},{72,6... | collective-permute-start | bytes 15368 | tf_op jit(solution)/shard_map/while/body/eval_jaxpr/ppermute | solution.py:25
  107.7 8.1 %collective-permute-start.2 = (f32[5,68,2]{2,1,0:T(8,128)S(1)}, f32[5,68,2]{2,1,0:T(8,128)S(1)}, u32[]{:S(2)}, u32[]{:S(2)}) collective-permute-start(f32[5,68,2]{2,1,0:T(8,128)S(1)} %get-tuple-element.232), channel_id=1, source_target_pairs={{1,0},{2,1},{3,2},{4,3},{5,4},{6,5},{7,6},{9,8},{10,9},{11,10},{12... | collective-permute-start | bytes 8168 | tf_op jit(solution)/shard_map/while/body/eval_jaxpr/ppermute | solution.py:25
  109.0 8.3 %collective-permute-start.3 = (f32[5,68,2]{2,1,0:T(8,128)S(1)}, f32[5,68,2]{2,1,0:T(8,128)S(1)}, u32[]{:S(2)}, u32[]{:S(2)}) collective-permute-start(f32[5,68,2]{2,1,0:T(8,128)S(1)} %get-tuple-element.233), channel_id=1, source_target_pairs={{0,1},{1,2},{2,3},{3,4},{4,5},{5,6},{6,7},{8,9},{9,10},{10,11},{11... | collective-permute-start | bytes 8168 | tf_op jit(solution)/shard_map/while/body/eval_jaxpr/ppermute | solution.py:22
  119.1 10.8 %collective-permute-start = (f32[5,2,128]{2,1,0:T(2,128)S(1)}, f32[5,2,128]{2,1,0:T(2,128)S(1)}, u32[]{:S(2)}, u32[]{:S(2)}) collective-permute-start(f32[5,2,128]{2,1,0:T(2,128)S(1)} %get-tuple-element.230), channel_id=1, source_target_pairs={{8,0},{16,8},{24,16},{32,24},{40,32},{48,40},{56,48},{64,56},{72,6... | collective-permute-start | bytes 15368 | tf_op jit(solution)/shard_map/while/body/eval_jaxpr/ppermute | solution.py:25
  131.1 8.1 %collective-permute-start.2 = (f32[5,68,2]{2,1,0:T(8,128)S(1)}, f32[5,68,2]{2,1,0:T(8,128)S(1)}, u32[]{:S(2)}, u32[]{:S(2)}) collective-permute-start(f32[5,68,2]{2,1,0:T(8,128)S(1)} %get-tuple-element.232), channel_id=1, source_target_pairs={{1,0},{2,1},{3,2},{4,3},{5,4},{6,5},{7,6},{9,8},{10,9},{11,10},{12... | collective-permute-start | bytes 8168 | tf_op jit(solution)/shard_map/while/body/eval_jaxpr/ppermute | solution.py:25
  132.4 8.3 %collective-permute-start.3 = (f32[5,68,2]{2,1,0:T(8,128)S(1)}, f32[5,68,2]{2,1,0:T(8,128)S(1)}, u32[]{:S(2)}, u32[]{:S(2)}) collective-permute-start(f32[5,68,2]{2,1,0:T(8,128)S(1)} %get-tuple-element.233), channel_id=1, source_target_pairs={{0,1},{1,2},{2,3},{3,4},{4,5},{5,6},{6,7},{8,9},{9,10},{10,11},{11... | collective-permute-start | bytes 8168 | tf_op jit(solution)/shard_map/while/body/eval_jaxpr/ppermute | solution.py:22
  142.5 10.8 %collective-permute-start = (f32[5,2,128]{2,1,0:T(2,128)S(1)}, f32[5,2,128]{2,1,0:T(2,128)S(1)}, u32[]{:S(2)}, u32[]{:S(2)}) collective-permute-start(f32[5,2,128]{2,1,0:T(2,128)S(1)} %get-tuple-element.230), channel_id=1, source_target_pairs={{8,0},{16,8},{24,16},{32,24},{40,32},{48,40},{56,48},{64,56},{72,6... | collective-permute-start | bytes 15368 | tf_op jit(solution)/shard_map/while/body/eval_jaxpr/ppermute | solution.py:25
  154.6 8.2 %collective-permute-start.2 = (f32[5,68,2]{2,1,0:T(8,128)S(1)}, f32[5,68,2]{2,1,0:T(8,128)S(1)}, u32[]{:S(2)}, u32[]{:S(2)}) collective-permute-start(f32[5,68,2]{2,1,0:T(8,128)S(1)} %get-tuple-element.232), channel_id=1, source_target_pairs={{1,0},{2,1},{3,2},{4,3},{5,4},{6,5},{7,6},{9,8},{10,9},{11,10},{12... | collective-permute-start | bytes 8168 | tf_op jit(solution)/shard_map/while/body/eval_jaxpr/ppermute | solution.py:25
  155.9 8.4 %collective-permute-start.3 = (f32[5,68,2]{2,1,0:T(8,128)S(1)}, f32[5,68,2]{2,1,0:T(8,128)S(1)}, u32[]{:S(2)}, u32[]{:S(2)}) collective-permute-start(f32[5,68,2]{2,1,0:T(8,128)S(1)} %get-tuple-element.233), channel_id=1, source_target_pairs={{0,1},{1,2},{2,3},{3,4},{4,5},{5,6},{6,7},{8,9},{9,10},{10,11},{11... | collective-permute-start | bytes 8168 | tf_op jit(solution)/shard_map/while/body/eval_jaxpr/ppermute | solution.py:22
  166.0 10.8 %collective-permute-start = (f32[5,2,128]{2,1,0:T(2,128)S(1)}, f32[5,2,128]{2,1,0:T(2,128)S(1)}, u32[]{:S(2)}, u32[]{:S(2)}) collective-permute-start(f32[5,2,128]{2,1,0:T(2,128)S(1)} %get-tuple-element.230), channel_id=1, source_target_pairs={{8,0},{16,8},{24,16},{32,24},{40,32},{48,40},{56,48},{64,56},{72,6... | collective-permute-start | bytes 15368 | tf_op jit(solution)/shard_map/while/body/eval_jaxpr/ppermute | solution.py:25
  178.1 8.1 %collective-permute-start.2 = (f32[5,68,2]{2,1,0:T(8,128)S(1)}, f32[5,68,2]{2,1,0:T(8,128)S(1)}, u32[]{:S(2)}, u32[]{:S(2)}) collective-permute-start(f32[5,68,2]{2,1,0:T(8,128)S(1)} %get-tuple-element.232), channel_id=1, source_target_pairs={{1,0},{2,1},{3,2},{4,3},{5,4},{6,5},{7,6},{9,8},{10,9},{11,10},{12... | collective-permute-start | bytes 8168 | tf_op jit(solution)/shard_map/while/body/eval_jaxpr/ppermute | solution.py:25
  179.4 8.3 %collective-permute-start.3 = (f32[5,68,2]{2,1,0:T(8,128)S(1)}, f32[5,68,2]{2,1,0:T(8,128)S(1)}, u32[]{:S(2)}, u32[]{:S(2)}) collective-permute-start(f32[5,68,2]{2,1,0:T(8,128)S(1)} %get-tuple-element.233), channel_id=1, source_target_pairs={{0,1},{1,2},{2,3},{3,4},{4,5},{5,6},{6,7},{8,9},{9,10},{10,11},{11... | collective-permute-start | bytes 8168 | tf_op jit(solution)/shard_map/while/body/eval_jaxpr/ppermute | solution.py:22
  189.5 10.8 %collective-permute-start = (f32[5,2,128]{2,1,0:T(2,128)S(1)}, f32[5,2,128]{2,1,0:T(2,128)S(1)}, u32[]{:S(2)}, u32[]{:S(2)}) collective-permute-start(f32[5,2,128]{2,1,0:T(2,128)S(1)} %get-tuple-element.230), channel_id=1, source_target_pairs={{8,0},{16,8},{24,16},{32,24},{40,32},{48,40},{56,48},{64,56},{72,6... | collective-permute-start | bytes 15368 | tf_op jit(solution)/shard_map/while/body/eval_jaxpr/ppermute | solution.py:25
  201.6 8.1 %collective-permute-start.2 = (f32[5,68,2]{2,1,0:T(8,128)S(1)}, f32[5,68,2]{2,1,0:T(8,128)S(1)}, u32[]{:S(2)}, u32[]{:S(2)}) collective-permute-start(f32[5,68,2]{2,1,0:T(8,128)S(1)} %get-tuple-element.232), channel_id=1, source_target_pairs={{1,0},{2,1},{3,2},{4,3},{5,4},{6,5},{7,6},{9,8},{10,9},{11,10},{12... | collective-permute-start | bytes 8168 | tf_op jit(solution)/shard_map/while/body/eval_jaxpr/ppermute | solution.py:25
  202.9 8.3 %collective-permute-start.3 = (f32[5,68,2]{2,1,0:T(8,128)S(1)}, f32[5,68,2]{2,1,0:T(8,128)S(1)}, u32[]{:S(2)}, u32[]{:S(2)}) collective-permute-start(f32[5,68,2]{2,1,0:T(8,128)S(1)} %get-tuple-element.233), channel_id=1, source_target_pairs={{0,1},{1,2},{2,3},{3,4},{4,5},{5,6},{6,7},{8,9},{9,10},{10,11},{11... | collective-permute-start | bytes 8168 | tf_op jit(solution)/shard_map/while/body/eval_jaxpr/ppermute | solution.py:22
  212.9 10.8 %collective-permute-start = (f32[5,2,128]{2,1,0:T(2,128)S(1)}, f32[5,2,128]{2,1,0:T(2,128)S(1)}, u32[]{:S(2)}, u32[]{:S(2)}) collective-permute-start(f32[5,2,128]{2,1,0:T(2,128)S(1)} %get-tuple-element.230), channel_id=1, source_target_pairs={{8,0},{16,8},{24,16},{32,24},{40,32},{48,40},{56,48},{64,56},{72,6... | collective-permute-start | bytes 15368 | tf_op jit(solution)/shard_map/while/body/eval_jaxpr/ppermute | solution.py:25
  225.0 8.1 %collective-permute-start.2 = (f32[5,68,2]{2,1,0:T(8,128)S(1)}, f32[5,68,2]{2,1,0:T(8,128)S(1)}, u32[]{:S(2)}, u32[]{:S(2)}) collective-permute-start(f32[5,68,2]{2,1,0:T(8,128)S(1)} %get-tuple-element.232), channel_id=1, source_target_pairs={{1,0},{2,1},{3,2},{4,3},{5,4},{6,5},{7,6},{9,8},{10,9},{11,10},{12... | collective-permute-start | bytes 8168 | tf_op jit(solution)/shard_map/while/body/eval_jaxpr/ppermute | solution.py:25
  226.3 8.3 %collective-permute-start.3 = (f32[5,68,2]{2,1,0:T(8,128)S(1)}, f32[5,68,2]{2,1,0:T(8,128)S(1)}, u32[]{:S(2)}, u32[]{:S(2)}) collective-permute-start(f32[5,68,2]{2,1,0:T(8,128)S(1)} %get-tuple-element.233), channel_id=1, source_target_pairs={{0,1},{1,2},{2,3},{3,4},{4,5},{5,6},{6,7},{8,9},{9,10},{10,11},{11... | collective-permute-start | bytes 8168 | tf_op jit(solution)/shard_map/while/body/eval_jaxpr/ppermute | solution.py:22
  236.4 10.8 %collective-permute-start = (f32[5,2,128]{2,1,0:T(2,128)S(1)}, f32[5,2,128]{2,1,0:T(2,128)S(1)}, u32[]{:S(2)}, u32[]{:S(2)}) collective-permute-start(f32[5,2,128]{2,1,0:T(2,128)S(1)} %get-tuple-element.230), channel_id=1, source_target_pairs={{8,0},{16,8},{24,16},{32,24},{40,32},{48,40},{56,48},{64,56},{72,6... | collective-permute-start | bytes 15368 | tf_op jit(solution)/shard_map/while/body/eval_jaxpr/ppermute | solution.py:25
  249.7 8.2 %collective-permute-start.3 = (f32[5,68,2]{2,1,0:T(8,128)S(1)}, f32[5,68,2]{2,1,0:T(8,128)S(1)}, u32[]{:S(2)}, u32[]{:S(2)}) collective-permute-start(f32[5,68,2]{2,1,0:T(8,128)S(1)} %get-tuple-element.233), channel_id=1, source_target_pairs={{0,1},{1,2},{2,3},{3,4},{4,5},{5,6},{6,7},{8,9},{9,10},{10,11},{11... | collective-permute-start | bytes 8168 | tf_op jit(solution)/shard_map/while/body/eval_jaxpr/ppermute | solution.py:22
  259.7 10.8 %collective-permute-start = (f32[5,2,128]{2,1,0:T(2,128)S(1)}, f32[5,2,128]{2,1,0:T(2,128)S(1)}, u32[]{:S(2)}, u32[]{:S(2)}) collective-permute-start(f32[5,2,128]{2,1,0:T(2,128)S(1)} %get-tuple-element.230), channel_id=1, source_target_pairs={{8,0},{16,8},{24,16},{32,24},{40,32},{48,40},{56,48},{64,56},{72,6... | collective-permute-start | bytes 15368 | tf_op jit(solution)/shard_map/while/body/eval_jaxpr/ppermute | solution.py:25
  273.1 8.2 %collective-permute-start.3 = (f32[5,68,2]{2,1,0:T(8,128)S(1)}, f32[5,68,2]{2,1,0:T(8,128)S(1)}, u32[]{:S(2)}, u32[]{:S(2)}) collective-permute-start(f32[5,68,2]{2,1,0:T(8,128)S(1)} %get-tuple-element.233), channel_id=1, source_target_pairs={{0,1},{1,2},{2,3},{3,4},{4,5},{5,6},{6,7},{8,9},{9,10},{10,11},{11... | collective-permute-start | bytes 8168 | tf_op jit(solution)/shard_map/while/body/eval_jaxpr/ppermute | solution.py:22
  283.0 10.8 %collective-permute-start = (f32[5,2,128]{2,1,0:T(2,128)S(1)}, f32[5,2,128]{2,1,0:T(2,128)S(1)}, u32[]{:S(2)}, u32[]{:S(2)}) collective-permute-start(f32[5,2,128]{2,1,0:T(2,128)S(1)} %get-tuple-element.230), channel_id=1, source_target_pairs={{8,0},{16,8},{24,16},{32,24},{40,32},{48,40},{56,48},{64,56},{72,6... | collective-permute-start | bytes 15368 | tf_op jit(solution)/shard_map/while/body/eval_jaxpr/ppermute | solution.py:25
  296.4 8.2 %collective-permute-start.3 = (f32[5,68,2]{2,1,0:T(8,128)S(1)}, f32[5,68,2]{2,1,0:T(8,128)S(1)}, u32[]{:S(2)}, u32[]{:S(2)}) collective-permute-start(f32[5,68,2]{2,1,0:T(8,128)S(1)} %get-tuple-element.233), channel_id=1, source_target_pairs={{0,1},{1,2},{2,3},{3,4},{4,5},{5,6},{6,7},{8,9},{9,10},{10,11},{11... | collective-permute-start | bytes 8168 | tf_op jit(solution)/shard_map/while/body/eval_jaxpr/ppermute | solution.py:22
  306.4 10.8 %collective-permute-start = (f32[5,2,128]{2,1,0:T(2,128)S(1)}, f32[5,2,128]{2,1,0:T(2,128)S(1)}, u32[]{:S(2)}, u32[]{:S(2)}) collective-permute-start(f32[5,2,128]{2,1,0:T(2,128)S(1)} %get-tuple-element.230), channel_id=1, source_target_pairs={{8,0},{16,8},{24,16},{32,24},{40,32},{48,40},{56,48},{64,56},{72,6... | collective-permute-start | bytes 15368 | tf_op jit(solution)/shard_map/while/body/eval_jaxpr/ppermute | solution.py:25
  319.7 8.2 %collective-permute-start.3 = (f32[5,68,2]{2,1,0:T(8,128)S(1)}, f32[5,68,2]{2,1,0:T(8,128)S(1)}, u32[]{:S(2)}, u32[]{:S(2)}) collective-permute-start(f32[5,68,2]{2,1,0:T(8,128)S(1)} %get-tuple-element.233), channel_id=1, source_target_pairs={{0,1},{1,2},{2,3},{3,4},{4,5},{5,6},{6,7},{8,9},{9,10},{10,11},{11... | collective-permute-start | bytes 8168 | tf_op jit(solution)/shard_map/while/body/eval_jaxpr/ppermute | solution.py:22
  329.7 10.8 %collective-permute-start = (f32[5,2,128]{2,1,0:T(2,128)S(1)}, f32[5,2,128]{2,1,0:T(2,128)S(1)}, u32[]{:S(2)}, u32[]{:S(2)}) collective-permute-start(f32[5,2,128]{2,1,0:T(2,128)S(1)} %get-tuple-element.230), channel_id=1, source_target_pairs={{8,0},{16,8},{24,16},{32,24},{40,32},{48,40},{56,48},{64,56},{72,6... | collective-permute-start | bytes 15368 | tf_op jit(solution)/shard_map/while/body/eval_jaxpr/ppermute | solution.py:25
  343.1 8.2 %collective-permute-start.3 = (f32[5,68,2]{2,1,0:T(8,128)S(1)}, f32[5,68,2]{2,1,0:T(8,128)S(1)}, u32[]{:S(2)}, u32[]{:S(2)}) collective-permute-start(f32[5,68,2]{2,1,0:T(8,128)S(1)} %get-tuple-element.233), channel_id=1, source_target_pairs={{0,1},{1,2},{2,3},{3,4},{4,5},{5,6},{6,7},{8,9},{9,10},{10,11},{11... | collective-permute-start | bytes 8168 | tf_op jit(solution)/shard_map/while/body/eval_jaxpr/ppermute | solution.py:22
  353.0 10.8 %collective-permute-start = (f32[5,2,128]{2,1,0:T(2,128)S(1)}, f32[5,2,128]{2,1,0:T(2,128)S(1)}, u32[]{:S(2)}, u32[]{:S(2)}) collective-permute-start(f32[5,2,128]{2,1,0:T(2,128)S(1)} %get-tuple-element.230), channel_id=1, source_target_pairs={{8,0},{16,8},{24,16},{32,24},{40,32},{48,40},{56,48},{64,56},{72,6... | collective-permute-start | bytes 15368 | tf_op jit(solution)/shard_map/while/body/eval_jaxpr/ppermute | solution.py:25
  366.4 8.2 %collective-permute-start.3 = (f32[5,68,2]{2,1,0:T(8,128)S(1)}, f32[5,68,2]{2,1,0:T(8,128)S(1)}, u32[]{:S(2)}, u32[]{:S(2)}) collective-permute-start(f32[5,68,2]{2,1,0:T(8,128)S(1)} %get-tuple-element.233), channel_id=1, source_target_pairs={{0,1},{1,2},{2,3},{3,4},{4,5},{5,6},{6,7},{8,9},{9,10},{10,11},{11... | collective-permute-start | bytes 8168 | tf_op jit(solution)/shard_map/while/body/eval_jaxpr/ppermute | solution.py:22
  376.4 10.8 %collective-permute-start = (f32[5,2,128]{2,1,0:T(2,128)S(1)}, f32[5,2,128]{2,1,0:T(2,128)S(1)}, u32[]{:S(2)}, u32[]{:S(2)}) collective-permute-start(f32[5,2,128]{2,1,0:T(2,128)S(1)} %get-tuple-element.230), channel_id=1, source_target_pairs={{8,0},{16,8},{24,16},{32,24},{40,32},{48,40},{56,48},{64,56},{72,6... | collective-permute-start | bytes 15368 | tf_op jit(solution)/shard_map/while/body/eval_jaxpr/ppermute | solution.py:25
  389.7 8.2 %collective-permute-start.3 = (f32[5,68,2]{2,1,0:T(8,128)S(1)}, f32[5,68,2]{2,1,0:T(8,128)S(1)}, u32[]{:S(2)}, u32[]{:S(2)}) collective-permute-start(f32[5,68,2]{2,1,0:T(8,128)S(1)} %get-tuple-element.233), channel_id=1, source_target_pairs={{0,1},{1,2},{2,3},{3,4},{4,5},{5,6},{6,7},{8,9},{9,10},{10,11},{11... | collective-permute-start | bytes 8168 | tf_op jit(solution)/shard_map/while/body/eval_jaxpr/ppermute | solution.py:22
  399.7 10.8 %collective-permute-start = (f32[5,2,128]{2,1,0:T(2,128)S(1)}, f32[5,2,128]{2,1,0:T(2,128)S(1)}, u32[]{:S(2)}, u32[]{:S(2)}) collective-permute-start(f32[5,2,128]{2,1,0:T(2,128)S(1)} %get-tuple-element.230), channel_id=1, source_target_pairs={{8,0},{16,8},{24,16},{32,24},{40,32},{48,40},{56,48},{64,56},{72,6... | collective-permute-start | bytes 15368 | tf_op jit(solution)/shard_map/while/body/eval_jaxpr/ppermute | solution.py:25
  413.1 8.2 %collective-permute-start.3 = (f32[5,68,2]{2,1,0:T(8,128)S(1)}, f32[5,68,2]{2,1,0:T(8,128)S(1)}, u32[]{:S(2)}, u32[]{:S(2)}) collective-permute-start(f32[5,68,2]{2,1,0:T(8,128)S(1)} %get-tuple-element.233), channel_id=1, source_target_pairs={{0,1},{1,2},{2,3},{3,4},{4,5},{5,6},{6,7},{8,9},{9,10},{10,11},{11... | collective-permute-start | bytes 8168 | tf_op jit(solution)/shard_map/while/body/eval_jaxpr/ppermute | solution.py:22
  423.1 10.8 %collective-permute-start = (f32[5,2,128]{2,1,0:T(2,128)S(1)}, f32[5,2,128]{2,1,0:T(2,128)S(1)}, u32[]{:S(2)}, u32[]{:S(2)}) collective-permute-start(f32[5,2,128]{2,1,0:T(2,128)S(1)} %get-tuple-element.230), channel_id=1, source_target_pairs={{8,0},{16,8},{24,16},{32,24},{40,32},{48,40},{56,48},{64,56},{72,6... | collective-permute-start | bytes 15368 | tf_op jit(solution)/shard_map/while/body/eval_jaxpr/ppermute | solution.py:25
  436.4 8.2 %collective-permute-start.3 = (f32[5,68,2]{2,1,0:T(8,128)S(1)}, f32[5,68,2]{2,1,0:T(8,128)S(1)}, u32[]{:S(2)}, u32[]{:S(2)}) collective-permute-start(f32[5,68,2]{2,1,0:T(8,128)S(1)} %get-tuple-element.233), channel_id=1, source_target_pairs={{0,1},{1,2},{2,3},{3,4},{4,5},{5,6},{6,7},{8,9},{9,10},{10,11},{11... | collective-permute-start | bytes 8168 | tf_op jit(solution)/shard_map/while/body/eval_jaxpr/ppermute | solution.py:22
  446.4 10.8 %collective-permute-start = (f32[5,2,128]{2,1,0:T(2,128)S(1)}, f32[5,2,128]{2,1,0:T(2,128)S(1)}, u32[]{:S(2)}, u32[]{:S(2)}) collective-permute-start(f32[5,2,128]{2,1,0:T(2,128)S(1)} %get-tuple-element.230), channel_id=1, source_target_pairs={{8,0},{16,8},{24,16},{32,24},{40,32},{48,40},{56,48},{64,56},{72,6... | collective-permute-start | bytes 15368 | tf_op jit(solution)/shard_map/while/body/eval_jaxpr/ppermute | solution.py:25
  459.8 8.2 %collective-permute-start.3 = (f32[5,68,2]{2,1,0:T(8,128)S(1)}, f32[5,68,2]{2,1,0:T(8,128)S(1)}, u32[]{:S(2)}, u32[]{:S(2)}) collective-permute-start(f32[5,68,2]{2,1,0:T(8,128)S(1)} %get-tuple-element.233), channel_id=1, source_target_pairs={{0,1},{1,2},{2,3},{3,4},{4,5},{5,6},{6,7},{8,9},{9,10},{10,11},{11... | collective-permute-start | bytes 8168 | tf_op jit(solution)/shard_map/while/body/eval_jaxpr/ppermute | solution.py:22
  469.7 10.8 %collective-permute-start = (f32[5,2,128]{2,1,0:T(2,128)S(1)}, f32[5,2,128]{2,1,0:T(2,128)S(1)}, u32[]{:S(2)}, u32[]{:S(2)}) collective-permute-start(f32[5,2,128]{2,1,0:T(2,128)S(1)} %get-tuple-element.230), channel_id=1, source_target_pairs={{8,0},{16,8},{24,16},{32,24},{40,32},{48,40},{56,48},{64,56},{72,6... | collective-permute-start | bytes 15368 | tf_op jit(solution)/shard_map/while/body/eval_jaxpr/ppermute | solution.py:25
  483.1 8.2 %collective-permute-start.3 = (f32[5,68,2]{2,1,0:T(8,128)S(1)}, f32[5,68,2]{2,1,0:T(8,128)S(1)}, u32[]{:S(2)}, u32[]{:S(2)}) collective-permute-start(f32[5,68,2]{2,1,0:T(8,128)S(1)} %get-tuple-element.233), channel_id=1, source_target_pairs={{0,1},{1,2},{2,3},{3,4},{4,5},{5,6},{6,7},{8,9},{9,10},{10,11},{11... | collective-permute-start | bytes 8168 | tf_op jit(solution)/shard_map/while/body/eval_jaxpr/ppermute | solution.py:22
  494.6 17.4 %collective-permute-start.8 = (bf16[7,8,128]{2,1,0:T(8,128)(2,1)S(1)}, bf16[7,8,128]{2,1,0:T(8,128)(2,1)S(1)}, u32[]{:S(2)}, u32[]{:S(2)}) collective-permute-start(bf16[7,8,128]{2,1,0:T(8,128)(2,1)S(1)} %get-tuple-element.150), channel_id=1, source_target_pairs={{16,0},{24,8},{32,16},{40,24},{48,32},{56,40},{64,48},{72,56},{80,... | collective-permute-start | bytes 43016 | tf_op jit(solution)/shard_map/ppermute | solution.py:33
  501.8 10.2 %collective-permute-start.9 = (bf16[7,8,128]{2,1,0:T(8,128)(2,1)S(1)}, bf16[7,8,128]{2,1,0:T(8,128)(2,1)S(1)}, u32[]{:S(2)}, u32[]{:S(2)}) collective-permute-start(bf16[7,8,128]{2,1,0:T(8,128)(2,1)S(1)} %get-tuple-element.149), channel_id=1, source_target_pairs={{8,0},{16,8},{24,16},{32,24},{40,32},{48,40},{56,48},{64,56},{72,6... | collective-permute-start | bytes 43016 | tf_op jit(solution)/shard_map/ppermute | solution.py:33
  510.0 8.7 %collective-permute-start.11 = (bf16[7,8,128]{2,1,0:T(8,128)(2,1)S(1)}, bf16[7,8,128]{2,1,0:T(8,128)(2,1)S(1)}, u32[]{:S(2)}, u32[]{:S(2)}) collective-permute-start(bf16[7,8,128]{2,1,0:T(8,128)(2,1)S(1)} %get-tuple-element.147), channel_id=1, source_target_pairs={{0,16},{8,24},{16,32},{24,40},{32,48},{40,56},{48,64},{56,72},{64,... | collective-permute-start | bytes 43016 | tf_op jit(solution)/shard_map/ppermute | solution.py:33
  (51 other events, 773.6 us)
where the time goes:
time: 539 us; the launch traced here: 536 us
  starting transfers between devices  381 us (71%)
  waiting for transfers between devices  91.7 us (17%)
  local copies, waits for them, and re-layouts  25.1 us (5%)
  other arithmetic  19.7 us (4%)
  blocking collectives  15.6 us (3%)
    ppermute x42, starting transfers between devices, extended(): lax.ppermute(lax.slice_in_dim(block, 0, width, axis=dim), axis, backward)  203 us
    ppermute x42, starting transfers between devices, extended(): lax.ppermute(lax.slice_in_dim(block, block.shape[dim] - width, None, axis...  161 us
    ppermute x42, waiting for transfers between devices, extended(): lax.ppermute(lax.slice_in_dim(block, block.shape[dim] - width, None, axis...  57.3 us
    ppermute x42, waiting for transfers between devices, extended(): lax.ppermute(lax.slice_in_dim(block, 0, width, axis=dim), axis, backward)  27.8 us
    ppermute x4, starting transfers between devices, from_behind(): lax.ppermute(value, axis, [(source, source + steps) for source in range(l...  17.2 us
    all_to_all x1, blocking collectives, body(): lax.all_to_all(ordered[None, None], 'server', split_axis=3, concat_axis=3...  15.6 us
    slice x20, local copies, waits for them, and re-layouts, trim_rim(): array[..., amount:array.shape[-2] - amount, amount:array.shape[-1] - amount]  13.8 us
  transfers between devices with their start and end apart: 88, of which 64 were waited for; matrix products, arithmetic and copies ran while one was open for 0% of the time, Pallas kernels for 0%

commit v1 on v0

v1 whole, which is shorter than its diff:
```python
import functools

import jax
import jax.numpy as jnp
from jax import lax
from jax.experimental import pallas as pl
from jax.experimental.pallas import tpu as pltpu
from jax.sharding import PartitionSpec as P

MESH = pl.DeviceIdType.MESH

CY, CX = 64, 128
ITERS = 20
HALO = 2 * ITERS
ROWS = CY + 2 * HALO
PAD = 8
FIELDS = 9
CAP, OFFSETS, BLOCKS, CROSS = 8, 5, 8, 4

RELAXATION = 0.1
STEP_SIZE = 0.3
DRAG_RATE = 1.0
FRAC_FLOOR = 0.3
KEEP_S = 1.0 / (1.0 + RELAXATION)
KEEP_V = 1.0 / (1.0 + STEP_SIZE * DRAG_RATE)
LOAD_SCALE = RELAXATION * 0.5 * KEEP_S
FORCE_SCALE = STEP_SIZE * KEEP_V * 0.25
WIND_SCALE = STEP_SIZE * KEEP_V
TINY = 1e-30

SIDE_ROWS = 3 * CY
CORNER_ROWS = 128
EDGE_ROWS = 368

SPATIAL = ((0, -1), (0, 1), (-1, 0), (1, 0), (-1, -1), (-1, 1), (1, -1), (1, 1))
AROUND = SPATIAL + ((-2, 0), (2, 0)) + tuple((0, k) for k in range(2, 7))


def rolled(x, amount):
    amount = amount % CX
    return x if amount == 0 else pltpu.roll(x, amount, 1)


def kernel(
    n_mp,
    n_server,
    vel_hbm,
    stress_hbm,
    wind_hbm,
    strength_hbm,
    mass_hbm,
    mask_hbm,
    send_list_hbm,
    block_index_hbm,
    span_slot_hbm,
    weights_hbm,
    state_hbm,
    written_ref,
    vel,
    stress,
    wind,
    strength,
    mass,
    mask,
    send_list,
    block_index,
    span_slot,
    weights,
    state,
    cells,
    moist,
    chosen,
    pressure,
    side_out,
    edge_out,
    corner_out,
    side_in,
    edge_in,
    corner_in,
    field_rows,
    rows_out,
    rows_in,
    rows_all,
    blocks_done,
    spans_out,
    spans_in,
    in_sem,
    weight_sem,
    state_sem,
    halo_send,
    halo_recv,
    rows_send,
    rows_recv,
    spans_send,
    spans_recv,
):
    me_y, me_x = lax.axis_index("mp"), lax.axis_index("server")

    def device(dy, dx):
        return (lax.rem(me_y + dy + n_mp, n_mp), lax.rem(me_x + dx + n_server, n_server))

    barrier = pltpu.get_barrier_semaphore()
    for dy, dx in AROUND:
        pl.semaphore_signal(barrier, inc=1, device_id=device(dy, dx), device_id_type=MESH)

    loads = [
        pltpu.make_async_copy(source, target, in_sem.at[i])
        for i, (source, target) in enumerate(
            (
                (vel_hbm, vel),
                (stress_hbm, stress),
                (wind_hbm, wind),
                (strength_hbm, strength),
                (mass_hbm, mass),
                (mask_hbm, mask),
                (send_list_hbm, send_list),
                (block_index_hbm, block_index),
                (span_slot_hbm, span_slot),
            )
        )
    ]
    for load in loads:
        load.start()
    weight_load = pltpu.make_async_copy(weights_hbm, weights, weight_sem)
    weight_load.start()
    for load in loads[:6]:
        load.wait()

    ice = mask[...].astype(jnp.float32)
    per_mass = ice / mass[...]
    own = [
        vel[0],
        vel[1],
        stress[0] + stress[1],
        stress[0] - stress[1],
        stress[2] * 2.0,
        strength[...] * ice * LOAD_SCALE,
        per_mass * FORCE_SCALE,
        wind[0] * per_mass * WIND_SCALE,
        wind[1] * per_mass * WIND_SCALE,
    ]
    lane = lax.broadcasted_iota(jnp.int32, (CY, CX), 1)
    spare = jnp.zeros((8, CX), jnp.float32)
    for f in range(FIELDS):
        cells[f, 0, PAD + HALO : PAD + HALO + CY] = own[f]
        for part in range(2):
            cells[f, part, 0:PAD] = spare
            cells[f, part, PAD + ROWS : PAD + ROWS + PAD] = spare
    edge_out[0] = jnp.concatenate([x[:HALO] for x in own] + [spare], axis=0).astype(jnp.bfloat16)
    edge_out[1] = jnp.concatenate([x[CY - HALO :] for x in own] + [spare], axis=0).astype(jnp.bfloat16)
    to_left, to_right = [], []
    for i in range(3):
        parts = [rolled(own[3 * k + i], 40 * k) for k in range(3)]
        to_left.append(jnp.where(lane < 40, parts[0], jnp.where(lane < 80, parts[1], parts[2])))
        to_right.append(jnp.where(lane >= 88, parts[0], jnp.where(lane < 40, parts[1], parts[2])))
    for side, packet in enumerate((to_left, to_right)):
        side_out[side] = jnp.concatenate(packet, axis=0).astype(jnp.bfloat16)
        corner_out[side] = jnp.concatenate([x[:HALO] for x in packet] + [spare], axis=0).astype(jnp.bfloat16)
        corner_out[2 + side] = jnp.concatenate([x[CY - HALO :] for x in packet] + [spare], axis=0).astype(jnp.bfloat16)

    pl.semaphore_wait(barrier, len(AROUND))

    sources = (
        side_out.at[0],
        side_out.at[1],
        edge_out.at[0],
        edge_out.at[1],
        corner_out.at[0],
        corner_out.at[1],
        corner_out.at[2],
        corner_out.at[3],
    )
    targets = (
        side_in.at[0],
        side_in.at[1],
        edge_in.at[0],
        edge_in.at[1],
        corner_in.at[0],
        corner_in.at[1],
        corner_in.at[2],
        corner_in.at[3],
    )
    halo = []
    for i, (dy, dx) in enumerate(SPATIAL):
        copy = pltpu.make_async_remote_copy(
            src_ref=sources[i],
            dst_ref=targets[i],
            send_sem=halo_send.at[i],
            recv_sem=halo_recv.at[i],
            device_id=device(dy, dx),
            device_id_type=MESH,
        )
        copy.start()
        halo.append(copy)
    for load in loads[6:]:
        load.wait()
    column = lax.broadcasted_iota(jnp.int32, (8, 8 * CY), 1) - CY * lax.broadcasted_iota(jnp.int32, (8, 8 * CY), 0)
    for offset in range(OFFSETS):
        picks = [
            (column == send_list[0, offset, 0, slot]).astype(jnp.float32) for slot in range(CAP)
        ]
        chosen[offset * 64 : (offset + 1) * 64] = jnp.concatenate(picks, axis=0).astype(jnp.bfloat16)
    for copy in halo:
        copy.wait()

    has_left = (me_x > 0).astype(jnp.float32)
    has_right = (me_x < n_server - 1).astype(jnp.float32)
    has_up = (me_y > 0).astype(jnp.float32)
    has_down = (me_y < n_mp - 1).astype(jnp.float32)
    top, low = PAD, PAD + HALO + CY
    for which, start, there in ((1, top, has_up), (0, low, has_down)):
        packet = edge_in[which].astype(jnp.float32) * there
        for f in range(FIELDS):
            cells[f, 0, start : start + HALO] = packet[f * HALO : (f + 1) * HALO]
    for right, left, start, count, there in (
        (side_in.at[0], side_in.at[1], PAD + HALO, CY, 1.0),
        (corner_in.at[2], corner_in.at[3], top, HALO, has_up),
        (corner_in.at[0], corner_in.at[1], low, HALO, has_down),
    ):
        packet_right = right[...].astype(jnp.float32) * (has_right * there)
        packet_left = left[...].astype(jnp.float32) * (has_left * there)
        spot = lax.broadcasted_iota(jnp.int32, (count, CX), 1)
        for i in range(3):
            from_right = packet_right[i * count : (i + 1) * count]
            from_left = packet_left[i * count : (i + 1) * count]
            for k in range(3):
                inside = (spot >= 40 * k) & (spot < 40 * k + 40)
                cells[3 * k + i, 1, start : start + count] = rolled(
                    jnp.where(inside, from_right, from_left), -40 * k
                )
    field_rows[6 * CY : 7 * CY] = mask[...].astype(jnp.bfloat16)
    field_rows[7 * CY : 8 * CY] = jnp.zeros((CY, CX), jnp.bfloat16)
    for part in range(2):
        moist[part] = jnp.where(cells[6, part] > 0.0, KEEP_V, 0.0)

    def ring(pair, step, first, last):
        a, b = (pltpu.roll(x, step % CX, 1) for x in pair)
        return (jnp.where(first, b, a), jnp.where(first, a, b)) if step == 1 else (jnp.where(last, b, a), jnp.where(last, a, b))

    def across(pair, first, last):
        before = ring(pair, 1, first, last)
        after = ring(pair, -1, first, last)
        return [y - x for x, y in zip(before, after)]

    def stresses(start, count, keep_pressure):
        spot = lax.broadcasted_iota(jnp.int32, (count, CX), 1)
        first, last = spot == 0, spot == CX - 1
        here, above, below = (pl.ds(start + d, count) for d in (0, -1, 1))
        u_x = across([cells[0, p, here] for p in range(2)], first, last)
        v_x = across([cells[1, p, here] for p in range(2)], first, last)
        for p in range(2):
            u_y = cells[0, p, below] - cells[0, p, above]
            v_y = cells[1, p, below] - cells[1, p, above]
            div, ten, shear = u_x[p] + v_y, u_x[p] - v_y, u_y + v_x[p]
            square = jnp.maximum(div * div + 0.25 * (ten * ten + shear * shear), TINY)
            deform = square * lax.rsqrt(square)
            bottom = deform + 1.0
            inverse = pl.reciprocal(bottom, approx=True)
            inverse = inverse * (2.0 - bottom * inverse)
            zeta = cells[5, p, here] * inverse
            one = zeta * (div - deform)
            two = (zeta * 0.25) * ten
            cells[2, p, here] = KEEP_S * cells[2, p, here] + (one + two)
            cells[3, p, here] = KEEP_S * cells[3, p, here] + (one - two)
            cells[4, p, here] = KEEP_S * cells[4, p, here] + (zeta * 0.5) * shear
            if keep_pressure and p == 0:
                pressure[pl.ds(start - PAD - HALO, count)] = zeta * deform * (1.0 / LOAD_SCALE)

    def velocities(start, count):
        spot = lax.broadcasted_iota(jnp.int32, (count, CX), 1)
        first, last = spot == 0, spot == CX - 1
        here, above, below = (pl.ds(start + d, count) for d in (0, -1, 1))
        p_x = across([cells[2, p, here] for p in range(2)], first, last)
        s_x = across([cells[4, p, here] for p in range(2)], first, last)
        for p in range(2):
            s_y = cells[4, p, below] - cells[4, p, above]
            m_y = cells[3, p, below] - cells[3, p, above]
            drag, keep = cells[6, p, here], moist[p, here]
            cells[0, p, here] = keep * cells[0, p, here] + ((p_x[p] + s_y) * drag + cells[7, p, here])
            cells[1, p, here] = keep * cells[1, p, here] + ((s_x[p] + m_y) * drag + cells[8, p, here])

    def subcycle(begin, end, inner, final=False):
        inside = range(HALO, HALO + CY, 8)
        for start in range(begin, end, 8):
            stresses(PAD + start, 8, final and start in inside)
        for start in range(begin + inner, end - inner, 8):
            velocities(PAD + start, 8)

    for stage in range(ITERS // 4):
        begin, end = 8 * stage, ROWS - 8 * stage

        def three(step, carry, begin=begin, end=end):
            subcycle(begin, end, 0)
            return carry

        lax.fori_loop(0, 3, three, 0)
        subcycle(begin, end, 8, stage == ITERS // 4 - 1)

    tile = slice(PAD + HALO, PAD + HALO + CY)
    plus, minus = cells[2, 0, tile], cells[3, 0, tile]
    results = (
        cells[0, 0, tile],
        cells[1, 0, tile],
        0.5 * (plus + minus),
        0.5 * (plus - minus),
        0.5 * cells[4, 0, tile],
    )
    for f, value in enumerate(results):
        state[f] = value
        field_rows[f * CY : (f + 1) * CY] = value.astype(jnp.bfloat16)
    field_rows[5 * CY : 6 * CY] = pressure[...].astype(jnp.bfloat16)
    state_store = pltpu.make_async_copy(state, state_hbm, state_sem)
    state_store.start()

    rows_copies = []
    for order, offset in enumerate((0, 1, 3, 4, 2)):
        packet = jnp.dot(
            chosen[offset * 64 : (offset + 1) * 64], field_rows[...], preferred_element_type=jnp.float32
        )
        if offset == 2:
            rows_all[offset * CAP : (offset + 1) * CAP] = packet.reshape(CAP, 8, CX)
            continue
        rows_out[order] = packet.astype(jnp.bfloat16)
        copy = pltpu.make_async_remote_copy(
            src_ref=rows_out.at[order],
            dst_ref=rows_in.at[order],
            send_sem=rows_send.at[order],
            recv_sem=rows_recv.at[order],
            device_id=device(offset - 2, 0),
            device_id_type=MESH,
        )
        copy.start()
        rows_copies.append((order, offset, copy))
    weight_load.wait()
    for order, offset, copy in rows_copies:
        copy.wait()
        rows_all[offset * CAP : (offset + 1) * CAP] = rows_in[order].astype(jnp.float32).reshape(CAP, 8, CX)

    for block in range(BLOCKS):
        total = jnp.zeros((8, CX), jnp.float32)
        for cross in range(CROSS):
            source = rows_all[block_index[0, 0, cross, block]].astype(jnp.bfloat16)
            total += jnp.dot(source, weights[0, 0, block, cross], preferred_element_type=jnp.float32)
        blocks_done[block] = total / jnp.maximum(total[6:7], FRAC_FLOOR)

    def for_span(span):
        found = jnp.zeros((8, CX), jnp.float32)
        for block in range(BLOCKS):
            found = jnp.where(span_slot[0, 0, block] == span, blocks_done[block], found)
        return found

    span_copies = []
    for hop in range(1, n_server):
        target = lax.rem(me_x + hop, n_server)
        spans_out[hop] = for_span(target)
        copy = pltpu.make_async_remote_copy(
            src_ref=spans_out.at[hop],
            dst_ref=spans_in.at[pl.ds(pl.multiple_of(me_x * 8, 8), 8)],
            send_sem=spans_send.at[hop],
            recv_sem=spans_recv.at[hop],
            device_id=(me_y, target),
            device_id_type=MESH,
        )
        copy.start()
        span_copies.append(copy)
    spans_in[pl.ds(pl.multiple_of(me_x * 8, 8), 8)] = for_span(me_x)
    for copy in span_copies:
        copy.wait()
    for f in range(6):
        written_ref[0, 0, f] = spans_in[pl.ds(f, n_server, stride=8)]
    state_store.wait()


def solution(mesh):
    n_mp, n_server = mesh.shape["mp"], mesh.shape["server"]
    placed = (
        P(None, "mp", "server"),
        P(None, "mp", "server"),
        P(None, "mp", "server"),
        P("mp", "server"),
        P("mp", "server"),
        P("mp", "server"),
        P("mp", "server", None, None),
        P("mp", "server", None, None),
        P("mp", "server", None),
        P("mp", "server", None, None, None, None),
    )
    f32, bf16 = jnp.float32, jnp.bfloat16
    far = pl.BlockSpec(memory_space=pltpu.HBM)

    def body(*arguments):
        arguments = list(arguments)
        arguments[6] = jnp.transpose(arguments[6], (0, 2, 1, 3))
        arguments[7] = jnp.transpose(arguments[7], (0, 1, 3, 2))
        return pl.pallas_call(
            functools.partial(kernel, n_mp, n_server),
            out_shape=(
                jax.ShapeDtypeStruct((5, CY, CX), f32),
                jax.ShapeDtypeStruct((1, 1, 6, 8, CX), f32),
            ),
            in_specs=[far] * 10,
            out_specs=(far, pl.BlockSpec(memory_space=pltpu.VMEM)),
            scratch_shapes=[
                pltpu.VMEM((2, CY, CX), f32),
                pltpu.VMEM((3, CY, CX), f32),
                pltpu.VMEM((2, CY, CX), f32),
                pltpu.VMEM((CY, CX), f32),
                pltpu.VMEM((CY, CX), f32),
                pltpu.VMEM((CY, CX), jnp.int32),
                pltpu.SMEM((1, OFFSETS, 1, CAP), jnp.int32),
                pltpu.SMEM((1, 1, CROSS, BLOCKS), jnp.int32),
                pltpu.SMEM((1, 1, BLOCKS), jnp.int32),
                pltpu.VMEM((1, 1, BLOCKS, CROSS, CX, CX), bf16),
                pltpu.VMEM((5, CY, CX), f32),
                pltpu.VMEM((FIELDS, 2, ROWS + 2 * PAD, CX), f32),
                pltpu.VMEM((2, ROWS + 2 * PAD, CX), f32),
                pltpu.VMEM((OFFSETS * 64, 8 * CY), bf16),
                pltpu.VMEM((CY, CX), f32),
                pltpu.VMEM((2, SIDE_ROWS, CX), bf16),
                pltpu.VMEM((2, EDGE_ROWS, CX), bf16),
                pltpu.VMEM((4, CORNER_ROWS, CX), bf16),
                pltpu.VMEM((2, SIDE_ROWS, CX), bf16),
                pltpu.VMEM((2, EDGE_ROWS, CX), bf16),
                pltpu.VMEM((4, CORNER_ROWS, CX), bf16),
                pltpu.VMEM((8 * CY, CX), bf16),
                pltpu.VMEM((4, 64, CX), bf16),
                pltpu.VMEM((4, 64, CX), bf16),
                pltpu.VMEM((OFFSETS * CAP, 8, CX), f32),
                pltpu.VMEM((BLOCKS, 8, CX), f32),
                pltpu.VMEM((8, 8, CX), f32),
                pltpu.VMEM((64, CX), f32),
                pltpu.SemaphoreType.DMA((9,)),
                pltpu.SemaphoreType.DMA,
                pltpu.SemaphoreType.DMA,
                pltpu.SemaphoreType.DMA((8,)),
                pltpu.SemaphoreType.DMA((8,)),
                pltpu.SemaphoreType.DMA((4,)),
                pltpu.SemaphoreType.DMA((4,)),
                pltpu.SemaphoreType.DMA((8,)),
                pltpu.SemaphoreType.DMA((8,)),
            ],
            compiler_params=pltpu.CompilerParams(
                collective_id=0, has_side_effects=True, vmem_limit_bytes=60 << 20
            ),
            name="ice",
        )(*arguments)

    return jax.shard_map(
        body,
        mesh=mesh,
        in_specs=placed,
        out_specs=(P(None, "mp", "server"), P("mp", "server", None, None, None)),
        check_vma=False,
    )
```

time: 539 us -> 42.5 us (0.08)
  the two profiles are of different devices: /device:TPU:33 before, /device:TPU:1 now
where the time goes in v1:
time: 42.5 us; the launch traced here: 42.3 us
  Pallas kernels  39.5 us (93%)
  local copies, waits for them, and re-layouts  2.21 us (5%)
  between operations  0.65 us (2%)
    pallas_call x1, Pallas kernels, body(): pl.pallas_call(functools.partial(kernel, n_mp, n_server), out_shape=(jax....  39.5 us
    unnamed x4, local copies, waits for them, and re-layouts  2.21 us

profile of v1, /device:TPU:1, one launch (start us, length us, event | category | flops | bytes accessed | tf_op | source)
XLA Modules:
  0.0 42.3 jit_solution(8937760137648158495)
XLA Ops:
  0.6 39.5 %ice.1 = (f32[5,64,128]{2,1,0:T(8,128)}, f32[1,1,6,8,128]{4,3,2,1,0:T(8,128)}) custom-call(f32[2,64,128]{2,1,0:T(8,128)} %vel_hbm.1, f32[3,64,128]{2,1,0:T(8,128)} %stress_hbm.1, f32[2,64,128]{2,1,0:T(8,128)} %wind_hbm.1, f32[64,128]{1,0:T(8,128)} %strength_hbm.1, f32[64,128]{1,0:T(8,128)} %mass_hbm.1, s32[64,128]{1,0:T(8,128)} %mask_hbm.1, ...), custom_call_target="tpu_custom_call" | custom-call | tf_op jit(solution)/shard_map/ice/pallas_call | solution.py:395
  40.1 0.0 copy-start
  40.1 1.6 %copy.14 = f32[5,64,128]{2,1,0:T(8,128)} copy(f32[5,64,128]{2,1,0:T(8,128)} %get-tuple-element.4) | data formatting | bytes 327680
  41.7 0.0 copy-done
  41.7 0.6 %copy.15 = f32[1,1,6,8,128]{4,3,2,1,0:T(8,128)} copy(f32[1,1,6,8,128]{4,3,2,1,0:T(8,128)S(1)} %copy-done) | data formatting | bytes 49152
Async XLA Ops:
  40.1 1.6 %copy-start = (f32[1,1,6,8,128]{4,3,2,1,0:T(8,128)S(1)}, f32[1,1,6,8,128]{4,3,2,1,0:T(8,128)}, u32[]{:S(2)}) copy-start(f32[1,1,6,8,128]{4,3,2,1,0:T(8,128)} %get-tuple-element.5) | copy-start | bytes 73732

commit v2 on v1

v2 whole, which is shorter than its diff:
```python
import functools

import jax
import jax.numpy as jnp
from jax import lax
from jax.experimental import pallas as pl
from jax.experimental.pallas import tpu as pltpu
from jax.sharding import PartitionSpec as P

MESH = pl.DeviceIdType.MESH

CY, CX = 64, 128
ITERS = 20
HALO = 2 * ITERS
ROWS = CY + 2 * HALO
PAD = 8
FIELDS = 9
CAP, OFFSETS, BLOCKS, CROSS = 8, 5, 8, 4

RELAXATION = 0.1
STEP_SIZE = 0.3
DRAG_RATE = 1.0
FRAC_FLOOR = 0.3
KEEP_S = 1.0 / (1.0 + RELAXATION)
KEEP_V = 1.0 / (1.0 + STEP_SIZE * DRAG_RATE)
LOAD_SCALE = RELAXATION * 0.5 * KEEP_S
FORCE_SCALE = STEP_SIZE * KEEP_V * 0.25
WIND_SCALE = STEP_SIZE * KEEP_V
TINY = 1e-30

OWN_LANE = HALO // 2
RIGHT_LANE = (HALO + CX) // 2
SIDE_ROWS = 3 * CY
CORNER_ROWS = 80
EDGE_ROWS = 368
WIDTHS = (40, 32, 24, 16, 8)
STARTS = (0, 40, 72, 96, 112)
PLACE, BACK, SIDE, CORNER = 0, 256, 384, 1152

SPATIAL = ((0, -1), (0, 1), (-1, 0), (1, 0), (-1, -1), (-1, 1), (1, -1), (1, 1))
AROUND = SPATIAL + ((-2, 0), (2, 0)) + tuple((0, k) for k in range(2, 7))


def ones_where(condition):
    return jnp.where(condition, 1.0, 0.0).astype(jnp.bfloat16)


def fill_packing(packing):
    row = lax.broadcasted_iota(jnp.int32, (CX, CX), 0)
    shift = lax.broadcasted_iota(jnp.int32, (CX, CX), 1) - row
    slots = [(HALO, HALO * k) for k in range(3)] + list(zip(WIDTHS, STARTS))
    for i, (width, start) in enumerate(slots):
        rows = slice(i * CX, (i + 1) * CX)
        packing[rows, :CX] = ones_where((shift == start) & (row < width))
        packing[rows, CX:] = ones_where((shift == start - CX + width) & (row >= CX - width))


def fill_placing(placing):
    row = lax.broadcasted_iota(jnp.int32, (CX, CX), 0)
    column = lax.broadcasted_iota(jnp.int32, (CX, CX), 1)
    forth, back = 2 * column - row, 2 * row - column
    slots = [(SIDE + 2 * CX * k, HALO, HALO * k, 0) for k in range(3)]
    slots += [(CORNER + 2 * CX * g, WIDTHS[g], STARTS[g], 4 * g) for g in range(5)]
    for odd in range(2):
        own = ones_where(forth == HALO - odd)
        for half in range(2):
            placing[half * CX : (half + 1) * CX, PLACE + odd * CX : PLACE + (odd + 1) * CX] = own
        placing[odd * CX : (odd + 1) * CX, BACK:SIDE] = ones_where(back == HALO - odd)
        for at, width, start, lane in slots:
            columns = slice(at + odd * CX, at + (odd + 1) * CX)
            for half, first in enumerate((lane, RIGHT_LANE)):
                inside = (column >= first) & (column < first + width // 2)
                placing[half * CX : (half + 1) * CX, columns] = ones_where((forth == 2 * first - start - odd) & inside)


def split(x):
    high = x.astype(jnp.bfloat16)
    return high, (x - high.astype(jnp.float32)).astype(jnp.bfloat16)


def picked(x, matrix):
    return jnp.dot(x, matrix, preferred_element_type=jnp.float32)


def kernel(
    n_mp,
    n_server,
    vel_hbm,
    stress_hbm,
    wind_hbm,
    strength_hbm,
    mass_hbm,
    mask_hbm,
    send_list_hbm,
    block_index_hbm,
    span_slot_hbm,
    weights_hbm,
    state_ref,
    written_ref,
    vel,
    stress,
    wind,
    strength,
    mass,
    mask,
    send_list,
    block_index,
    span_slot,
    weights,
    packing,
    placing,
    cells,
    moist,
    chosen,
    pressure,
    side_out,
    edge_out,
    corner_out,
    side_in,
    edge_in,
    corner_in,
    field_rows,
    rows_out,
    rows_in,
    rows_all,
    blocks_done,
    spans_out,
    spans_in,
    in_sem,
    weight_sem,
    halo_send,
    halo_recv,
    rows_send,
    rows_recv,
    spans_send,
    spans_recv,
):
    me_y, me_x = lax.axis_index("mp"), lax.axis_index("server")

    def device(dy, dx):
        return (lax.rem(me_y + dy + n_mp, n_mp), lax.rem(me_x + dx + n_server, n_server))

    barrier = pltpu.get_barrier_semaphore()
    for dy, dx in AROUND:
        pl.semaphore_signal(barrier, inc=1, device_id=device(dy, dx), device_id_type=MESH)

    loads = [
        pltpu.make_async_copy(source, target, in_sem.at[i])
        for i, (source, target) in enumerate(
            (
                (vel_hbm, vel),
                (stress_hbm, stress),
                (wind_hbm, wind),
                (strength_hbm, strength),
                (mass_hbm, mass),
                (mask_hbm, mask),
                (send_list_hbm, send_list),
                (block_index_hbm, block_index),
                (span_slot_hbm, span_slot),
            )
        )
    ]
    for load in loads:
        load.start()
    weight_load = pltpu.make_async_copy(weights_hbm, weights, weight_sem)
    weight_load.start()
    fill_packing(packing)
    for load in loads[:6]:
        load.wait()

    ice = mask[...].astype(jnp.float32)
    per_mass = ice / mass[...]
    own = [
        vel[0],
        vel[1],
        stress[0] + stress[1],
        stress[0] - stress[1],
        stress[2] * 2.0,
        strength[...] * ice * LOAD_SCALE,
        per_mass * FORCE_SCALE,
        wind[0] * per_mass * WIND_SCALE,
        wind[1] * per_mass * WIND_SCALE,
    ]
    spare = jnp.zeros((8, CX), jnp.float32)
    edge_out[0] = jnp.concatenate([x[:HALO] for x in own] + [spare], axis=0).astype(jnp.bfloat16)
    edge_out[1] = jnp.concatenate([x[CY - HALO :] for x in own] + [spare], axis=0).astype(jnp.bfloat16)
    halo = [
        pltpu.make_async_remote_copy(
            src_ref=source,
            dst_ref=target,
            send_sem=halo_send.at[i],
            recv_sem=halo_recv.at[i],
            device_id=device(*SPATIAL[i]),
            device_id_type=MESH,
        )
        for i, (source, target) in enumerate(
            [(side_out.at[i], side_in.at[i]) for i in range(2)]
            + [(edge_out.at[i], edge_in.at[i]) for i in range(2)]
            + [(corner_out.at[i], corner_in.at[i]) for i in range(4)]
        )
    ]
    pl.semaphore_wait(barrier, len(AROUND))
    for i in (2, 3):
        halo[i].start()

    highs = [split(x) for x in own]
    sides = jnp.concatenate(
        [jnp.concatenate([highs[3 * k + i][0] for k in range(3)], axis=1) for i in range(3)], axis=0
    )
    packets = picked(sides, packing[: 3 * CX]).astype(jnp.bfloat16)
    for i in range(2):
        side_out[i] = packets[:, i * CX : (i + 1) * CX]
        halo[i].start()
    ends = []
    for edge in range(2):
        groups = [
            jnp.concatenate([x[8 * g : 8 * g + 8] if edge == 0 else x[CY - 8 - 8 * g : CY - 8 * g] for x in own], axis=0)
            for g in range(5)
        ]
        ends.append(jnp.concatenate([jnp.concatenate([x, spare], axis=0) for x in groups], axis=1))
    corners = picked(jnp.concatenate(ends, axis=0).astype(jnp.bfloat16), packing[3 * CX :]).astype(jnp.bfloat16)
    for i in range(4):
        corner_out[i] = corners[CORNER_ROWS * (i // 2) : CORNER_ROWS * (i // 2 + 1), CX * (i % 2) : CX * (i % 2 + 1)]
        halo[4 + i].start()

    for f in range(FIELDS):
        for part in range(2):
            cells[f, part, 0:PAD] = spare
            cells[f, part, PAD + ROWS : PAD + ROWS + PAD] = spare
    fill_placing(placing)
    for f in range(FIELDS):
        placed = picked(jnp.concatenate(highs[f], axis=1), placing[:, PLACE:BACK])
        for part in range(2):
            cells[f, part, PAD + HALO : PAD + HALO + CY] = placed[:, part * CX : (part + 1) * CX]

    for load in loads[6:]:
        load.wait()
    column = lax.broadcasted_iota(jnp.int32, (8, 8 * CY), 1) - CY * lax.broadcasted_iota(jnp.int32, (8, 8 * CY), 0)
    for offset in range(OFFSETS):
        picks = [
            (column == send_list[0, offset, 0, slot]).astype(jnp.float32) for slot in range(CAP)
        ]
        chosen[offset * 64 : (offset + 1) * 64] = jnp.concatenate(picks, axis=0).astype(jnp.bfloat16)
    has_left = (me_x > 0).astype(jnp.float32)
    has_right = (me_x < n_server - 1).astype(jnp.float32)
    has_up = (me_y > 0).astype(jnp.float32)
    has_down = (me_y < n_mp - 1).astype(jnp.float32)

    def kept(ref, there):
        return (ref[...].astype(jnp.float32) * there).astype(jnp.bfloat16)

    top, low = PAD, PAD + HALO + CY
    halo[0].wait_recv()
    halo[1].wait_recv()
    beside = jnp.concatenate([kept(side_in.at[1], has_left), kept(side_in.at[0], has_right)], axis=1)
    for k in range(3):
        found = picked(beside, placing[:, SIDE + 2 * CX * k : SIDE + 2 * CX * (k + 1)])
        for i in range(3):
            for part in range(2):
                cells[3 * k + i, part, PAD + HALO : low] += found[i * CY : (i + 1) * CY, part * CX : (part + 1) * CX]
    for which, start, there in ((1, top, has_up), (0, low, has_down)):
        halo[2 + which].wait_recv()
        found = picked(kept(edge_in.at[which], there), placing[:CX, PLACE:BACK])
        for f in range(FIELDS):
            for part in range(2):
                cells[f, part, start : start + HALO] = found[f * HALO : (f + 1) * HALO, part * CX : (part + 1) * CX]
    for copy in halo[4:]:
        copy.wait_recv()
    for from_left, from_right, start, there in ((3, 2, top, has_up), (1, 0, low, has_down)):
        beyond = jnp.concatenate(
            [kept(corner_in.at[from_left], has_left * there), kept(corner_in.at[from_right], has_right * there)], axis=1
        )
        for g in range(5):
            found = picked(beyond, placing[:, CORNER + 2 * CX * g : CORNER + 2 * CX * (g + 1)])
            at = start + (HALO - 8 - 8 * g if start == top else 8 * g)
            for f in range(FIELDS):
                for part in range(2):
                    cells[f, part, at : at + 8] += found[f * 8 : (f + 1) * 8, part * CX : (part + 1) * CX]
    field_rows[6 * CY : 7 * CY] = mask[...].astype(jnp.bfloat16)
    field_rows[7 * CY : 8 * CY] = jnp.zeros((CY, CX), jnp.bfloat16)
    for part in range(2):
        moist[part] = jnp.where(cells[6, part] > 0.0, KEEP_V, 0.0)

    def across(even, odd):
        return odd - pltpu.roll(odd, 1, 1), pltpu.roll(even, CX - 1, 1) - even

    def stresses(start, count, keep_pressure):
        here, above, below = (pl.ds(start + d, count) for d in (0, -1, 1))
        u_x = across(*(cells[0, p, here] for p in range(2)))
        v_x = across(*(cells[1, p, here] for p in range(2)))
        for p in range(2):
            u_y = cells[0, p, below] - cells[0, p, above]
            v_y = cells[1, p, below] - cells[1, p, above]
            div, ten, shear = u_x[p] + v_y, u_x[p] - v_y, u_y + v_x[p]
            square = jnp.maximum(div * div + 0.25 * (ten * ten + shear * shear), TINY)
            deform = square * lax.rsqrt(square)
            bottom = deform + 1.0
            inverse = pl.reciprocal(bottom, approx=True)
            zeta = cells[5, p, here] * inverse
            one = zeta * (div - deform)
            two = (zeta * 0.25) * ten
            cells[2, p, here] = KEEP_S * cells[2, p, here] + (one + two)
            cells[3, p, here] = KEEP_S * cells[3, p, here] + (one - two)
            cells[4, p, here] = KEEP_S * cells[4, p, here] + (zeta * 0.5) * shear
            if keep_pressure:
                pressure[p, pl.ds(start - PAD - HALO, count)] = zeta * deform * (1.0 / LOAD_SCALE)

    def velocities(start, count):
        here, above, below = (pl.ds(start + d, count) for d in (0, -1, 1))
        p_x = across(*(cells[2, p, here] for p in range(2)))
        s_x = across(*(cells[4, p, here] for p in range(2)))
        for p in range(2):
            s_y = cells[4, p, below] - cells[4, p, above]
            m_y = cells[3, p, below] - cells[3, p, above]
            drag, keep = cells[6, p, here], moist[p, here]
            cells[0, p, here] = keep * cells[0, p, here] + ((p_x[p] + s_y) * drag + cells[7, p, here])
            cells[1, p, here] = keep * cells[1, p, here] + ((s_x[p] + m_y) * drag + cells[8, p, here])

    wave = []
    for step in range(ITERS):
        first, last, inner = step // 4, ROWS // 8 - step // 4, int(step % 4 == 3)
        wave += [(6 * step + group, 1, step, group) for group in range(first, last)]
        wave += [(6 * step + group + 3, 0, step, group) for group in range(first + inner, last - inner)]
    for _, is_stress, step, group in sorted(wave):
        if is_stress:
            stresses(PAD + 8 * group, 8, step == ITERS - 1 and HALO <= 8 * group < HALO + CY)
        else:
            velocities(PAD + 8 * group, 8)

    tile = slice(PAD + HALO, PAD + HALO + CY)

    def results(part):
        plus, minus = cells[2, part, tile], cells[3, part, tile]
        yield cells[0, part, tile]
        yield cells[1, part, tile]
        yield 0.5 * (plus + minus)
        yield 0.5 * (plus - minus)
        yield 0.5 * cells[4, part, tile]

    back = placing[:, BACK:SIDE]
    rests = []
    for f, pair in enumerate(zip(results(0), results(1))):
        high, rest = zip(*(split(x) for x in pair))
        rests.append(rest)
        rounded = picked(jnp.concatenate(high, axis=1), back)
        state_ref[f] = rounded
        field_rows[f * CY : (f + 1) * CY] = rounded.astype(jnp.bfloat16)
    ends = jnp.concatenate([pressure[p].astype(jnp.bfloat16) for p in range(2)], axis=1)
    field_rows[5 * CY : 6 * CY] = picked(ends, back).astype(jnp.bfloat16)

    rows_copies = []
    for order, offset in enumerate((0, 1, 3, 4, 2)):
        packet = jnp.dot(
            chosen[offset * 64 : (offset + 1) * 64], field_rows[...], preferred_element_type=jnp.float32
        )
        if offset == 2:
            rows_all[offset * CAP : (offset + 1) * CAP] = packet.reshape(CAP, 8, CX)
            continue
        rows_out[order] = packet.astype(jnp.bfloat16)
        copy = pltpu.make_async_remote_copy(
            src_ref=rows_out.at[order],
            dst_ref=rows_in.at[order],
            send_sem=rows_send.at[order],
            recv_sem=rows_recv.at[order],
            device_id=device(offset - 2, 0),
            device_id_type=MESH,
        )
        copy.start()
        rows_copies.append((order, offset, copy))
    for f, rest in enumerate(rests):
        state_ref[f] += picked(jnp.concatenate(rest, axis=1), back)
    weight_load.wait()
    for order, offset, copy in rows_copies:
        copy.wait_recv()
        rows_all[offset * CAP : (offset + 1) * CAP] = rows_in[order].astype(jnp.float32).reshape(CAP, 8, CX)

    for block in range(BLOCKS):
        total = jnp.zeros((8, CX), jnp.float32)
        for cross in range(CROSS):
            source = rows_all[block_index[0, 0, cross, block]].astype(jnp.bfloat16)
            total += jnp.dot(source, weights[0, 0, block, cross], preferred_element_type=jnp.float32)
        blocks_done[block] = total / jnp.maximum(total[6:7], FRAC_FLOOR)

    def for_span(span):
        found = jnp.zeros((8, CX), jnp.float32)
        for block in range(BLOCKS):
            found = jnp.where(span_slot[0, 0, block] == span, blocks_done[block], found)
        return found

    span_copies = []
    for hop in range(1, n_server):
        target = lax.rem(me_x + hop, n_server)
        spans_out[hop] = for_span(target)
        copy = pltpu.make_async_remote_copy(
            src_ref=spans_out.at[hop],
            dst_ref=spans_in.at[pl.ds(pl.multiple_of(me_x * 8, 8), 8)],
            send_sem=spans_send.at[hop],
            recv_sem=spans_recv.at[hop],
            device_id=(me_y, target),
            device_id_type=MESH,
        )
        copy.start()
        span_copies.append(copy)
    spans_in[pl.ds(pl.multiple_of(me_x * 8, 8), 8)] = for_span(me_x)
    for copy in span_copies:
        copy.wait_recv()
    for f in range(6):
        written_ref[0, 0, f] = spans_in[pl.ds(f, n_server, stride=8)]
    for copy in halo + [copy for _, _, copy in rows_copies] + span_copies:
        copy.wait_send()


def solution(mesh):
    n_mp, n_server = mesh.shape["mp"], mesh.shape["server"]
    placed = (
        P(None, "mp", "server"),
        P(None, "mp", "server"),
        P(None, "mp", "server"),
        P("mp", "server"),
        P("mp", "server"),
        P("mp", "server"),
        P("mp", "server", None, None),
        P("mp", "server", None, None),
        P("mp", "server", None),
        P("mp", "server", None, None, None, None),
    )
    f32, bf16 = jnp.float32, jnp.bfloat16
    far = pl.BlockSpec(memory_space=pltpu.HBM)

    def body(*arguments):
        arguments = list(arguments)
        arguments[6] = jnp.transpose(arguments[6], (0, 2, 1, 3))
        arguments[7] = jnp.transpose(arguments[7], (0, 1, 3, 2))
        return pl.pallas_call(
            functools.partial(kernel, n_mp, n_server),
            out_shape=(
                pltpu.VMEM((5, CY, CX), f32),
                pltpu.VMEM((1, 1, 6, 8, CX), f32),
            ),
            in_specs=[far] * 10,
            out_specs=[pl.BlockSpec(memory_space=pltpu.VMEM)] * 2,
            scratch_shapes=[
                pltpu.VMEM((2, CY, CX), f32),
                pltpu.VMEM((3, CY, CX), f32),
                pltpu.VMEM((2, CY, CX), f32),
                pltpu.VMEM((CY, CX), f32),
                pltpu.VMEM((CY, CX), f32),
                pltpu.VMEM((CY, CX), jnp.int32),
                pltpu.SMEM((1, OFFSETS, 1, CAP), jnp.int32),
                pltpu.SMEM((1, 1, CROSS, BLOCKS), jnp.int32),
                pltpu.SMEM((1, 1, BLOCKS), jnp.int32),
                pltpu.VMEM((1, 1, BLOCKS, CROSS, CX, CX), bf16),
                pltpu.VMEM((8 * CX, 2 * CX), bf16),
                pltpu.VMEM((2 * CX, CORNER + 10 * CX), bf16),
                pltpu.VMEM((FIELDS, 2, ROWS + 2 * PAD, CX), f32),
                pltpu.VMEM((2, ROWS + 2 * PAD, CX), f32),
                pltpu.VMEM((OFFSETS * 64, 8 * CY), bf16),
                pltpu.VMEM((2, CY, CX), f32),
                pltpu.VMEM((2, SIDE_ROWS, CX), bf16),
                pltpu.VMEM((2, EDGE_ROWS, CX), bf16),
                pltpu.VMEM((4, CORNER_ROWS, CX), bf16),
                pltpu.VMEM((2, SIDE_ROWS, CX), bf16),
                pltpu.VMEM((2, EDGE_ROWS, CX), bf16),
                pltpu.VMEM((4, CORNER_ROWS, CX), bf16),
                pltpu.VMEM((8 * CY, CX), bf16),
                pltpu.VMEM((4, 64, CX), bf16),
                pltpu.VMEM((4, 64, CX), bf16),
                pltpu.VMEM((OFFSETS * CAP, 8, CX), f32),
                pltpu.VMEM((BLOCKS, 8, CX), f32),
                pltpu.VMEM((8, 8, CX), f32),
                pltpu.VMEM((64, CX), f32),
                pltpu.SemaphoreType.DMA((9,)),
                pltpu.SemaphoreType.DMA,
                pltpu.SemaphoreType.DMA((8,)),
                pltpu.SemaphoreType.DMA((8,)),
                pltpu.SemaphoreType.DMA((4,)),
                pltpu.SemaphoreType.DMA((4,)),
                pltpu.SemaphoreType.DMA((8,)),
                pltpu.SemaphoreType.DMA((8,)),
            ],
            compiler_params=pltpu.CompilerParams(
                collective_id=0, has_side_effects=True, vmem_limit_bytes=60 << 20
            ),
            name="ice",
        )(*arguments)

    return jax.shard_map(
        body,
        mesh=mesh,
        in_specs=placed,
        out_specs=(P(None, "mp", "server"), P("mp", "server", None, None, None)),
        check_vma=False,
    )
```

time: 42.5 us -> 38.6 us (0.908)
  Pallas kernels: 39.5 us -> 36.5 us
  local copies, waits for them, and re-layouts: 2.21 us -> 1.28 us
    pallas_call x1, Pallas kernels: 39.5 us -> 36.5 us  [body(): pl.pallas_call(functools.partial(kernel, n_mp, n_server), out_shape=(pltp...]
    unnamed x4 -> x2, local copies, waits for them, and re-layouts: 2.21 us -> 1.28 us
where the time goes in v2:
time: 38.6 us; the launch traced here: 38.4 us
  Pallas kernels  36.5 us (95%)
  local copies, waits for them, and re-layouts  1.28 us (3%)
  between operations  0.64 us (2%)
    pallas_call x1, Pallas kernels, body(): pl.pallas_call(functools.partial(kernel, n_mp, n_server), out_shape=(pltp...  36.5 us
    unnamed x2, local copies, waits for them, and re-layouts  1.28 us

profile of v2, /device:TPU:1, one launch (start us, length us, event | category | flops | bytes accessed | tf_op | source)
XLA Modules:
  0.0 38.4 jit_solution(16997148765256733878)
XLA Ops:
  0.6 36.5 %ice.1 = (f32[5,64,128]{2,1,0:T(8,128)S(1)}, f32[1,1,6,8,128]{4,3,2,1,0:T(8,128)S(1)}) custom-call(f32[2,64,128]{2,1,0:T(8,128)} %vel_hbm.1, f32[3,64,128]{2,1,0:T(8,128)} %stress_hbm.1, f32[2,64,128]{2,1,0:T(8,128)} %wind_hbm.1, f32[64,128]{1,0:T(8,128)} %strength_hbm.1, f32[64,128]{1,0:T(8,128)} %mass_hbm.1, s32[64,128]{1,0:T(8,128)} %mask_hbm.1, ...), custom_call_target="tpu_custom_call" | custom-call | tf_op jit(solution)/shard_map/ice/pallas_call | solution.py:434
  37.2 0.7 %copy.14 = f32[5,64,128]{2,1,0:T(8,128)} copy(f32[5,64,128]{2,1,0:T(8,128)S(1)} %get-tuple-element.2) | data formatting | bytes 327680
  37.8 0.6 %copy.15 = f32[1,1,6,8,128]{4,3,2,1,0:T(8,128)} copy(f32[1,1,6,8,128]{4,3,2,1,0:T(8,128)S(1)} %get-tuple-element.3) | data formatting | bytes 49152

commit v3 on v2

--- a/solution.py
+++ b/solution.py
@@ -140,9 +140,29 @@
     def device(dy, dx):
         return (lax.rem(me_y + dy + n_mp, n_mp), lax.rem(me_x + dx + n_server, n_server))
 
+    def inside(dy, dx):
+        found = None
+        for step, at, count in ((dy, me_y, n_mp), (dx, me_x, n_server)):
+            if step:
+                there = at >= -step if step < 0 else at < count - step
+                found = there if found is None else found & there
+        return found
+
+    def where_inside(dy, dx, action):
+        there = inside(dy, dx)
+        action() if there is None else pl.when(there)(action)
+
     barrier = pltpu.get_barrier_semaphore()
+    greeted = jnp.int32(0)
     for dy, dx in AROUND:
-        pl.semaphore_signal(barrier, inc=1, device_id=device(dy, dx), device_id_type=MESH)
+        where_inside(
+            dy,
+            0,
+            lambda dy=dy, dx=dx: pl.semaphore_signal(
+                barrier, inc=1, device_id=device(dy, dx), device_id_type=MESH
+            ),
+        )
+        greeted = greeted + (1 if dy == 0 else inside(dy, 0).astype(jnp.int32))
 
     loads = [
         pltpu.make_async_copy(source, target, in_sem.at[i])
@@ -199,9 +219,16 @@
             + [(corner_out.at[i], corner_in.at[i]) for i in range(4)]
         )
     ]
-    pl.semaphore_wait(barrier, len(AROUND))
+    pl.semaphore_wait(barrier, greeted)
+
+    def send_halo(i):
+        where_inside(*SPATIAL[i], lambda: halo[i].start())
+
+    def receive_halo(i):
+        where_inside(*(-step for step in SPATIAL[i]), lambda: halo[i].wait_recv())
+
     for i in (2, 3):
-        halo[i].start()
+        send_halo(i)
 
     highs = [split(x) for x in own]
     sides = jnp.concatenate(
@@ -210,7 +237,7 @@
     packets = picked(sides, packing[: 3 * CX]).astype(jnp.bfloat16)
     for i in range(2):
         side_out[i] = packets[:, i * CX : (i + 1) * CX]
-        halo[i].start()
+        send_halo(i)
     ends = []
     for edge in range(2):
         groups = [
@@ -221,7 +248,7 @@
     corners = picked(jnp.concatenate(ends, axis=0).astype(jnp.bfloat16), packing[3 * CX :]).astype(jnp.bfloat16)
     for i in range(4):
         corner_out[i] = corners[CORNER_ROWS * (i // 2) : CORNER_ROWS * (i // 2 + 1), CX * (i % 2) : CX * (i % 2 + 1)]
-        halo[4 + i].start()
+        send_halo(4 + i)
 
     for f in range(FIELDS):
         for part in range(2):
@@ -241,17 +268,15 @@
             (column == send_list[0, offset, 0, slot]).astype(jnp.float32) for slot in range(CAP)
         ]
         chosen[offset * 64 : (offset + 1) * 64] = jnp.concatenate(picks, axis=0).astype(jnp.bfloat16)
-    has_left = (me_x > 0).astype(jnp.float32)
-    has_right = (me_x < n_server - 1).astype(jnp.float32)
-    has_up = (me_y > 0).astype(jnp.float32)
-    has_down = (me_y < n_mp - 1).astype(jnp.float32)
+    has_left, has_right = me_x > 0, me_x < n_server - 1
+    has_up, has_down = me_y > 0, me_y < n_mp - 1
 
     def kept(ref, there):
-        return (ref[...].astype(jnp.float32) * there).astype(jnp.bfloat16)
+        return jnp.where(there, ref[...].astype(jnp.float32), 0.0).astype(jnp.bfloat16)
 
     top, low = PAD, PAD + HALO + CY
-    halo[0].wait_recv()
-    halo[1].wait_recv()
+    receive_halo(0)
+    receive_halo(1)
     beside = jnp.concatenate([kept(side_in.at[1], has_left), kept(side_in.at[0], has_right)], axis=1)
     for k in range(3):
         found = picked(beside, placing[:, SIDE + 2 * CX * k : SIDE + 2 * CX * (k + 1)])
@@ -259,16 +284,16 @@
             for part in range(2):
                 cells[3 * k + i, part, PAD + HALO : low] += found[i * CY : (i + 1) * CY, part * CX : (part + 1) * CX]
     for which, start, there in ((1, top, has_up), (0, low, has_down)):
-        halo[2 + which].wait_recv()
+        receive_halo(2 + which)
         found = picked(kept(edge_in.at[which], there), placing[:CX, PLACE:BACK])
         for f in range(FIELDS):
             for part in range(2):
                 cells[f, part, start : start + HALO] = found[f * HALO : (f + 1) * HALO, part * CX : (part + 1) * CX]
-    for copy in halo[4:]:
-        copy.wait_recv()
+    for i in range(4, 8):
+        receive_halo(i)
     for from_left, from_right, start, there in ((3, 2, top, has_up), (1, 0, low, has_down)):
         beyond = jnp.concatenate(
-            [kept(corner_in.at[from_left], has_left * there), kept(corner_in.at[from_right], has_right * there)], axis=1
+            [kept(corner_in.at[from_left], has_left & there), kept(corner_in.at[from_right], has_right & there)], axis=1
         )
         for g in range(5):
             found = picked(beyond, placing[:, CORNER + 2 * CX * g : CORNER + 2 * CX * (g + 1)])
@@ -365,20 +390,20 @@
             device_id=device(offset - 2, 0),
             device_id_type=MESH,
         )
-        copy.start()
+        where_inside(offset - 2, 0, copy.start)
         rows_copies.append((order, offset, copy))
     for f, rest in enumerate(rests):
         state_ref[f] += picked(jnp.concatenate(rest, axis=1), back)
     weight_load.wait()
     for order, offset, copy in rows_copies:
-        copy.wait_recv()
+        where_inside(2 - offset, 0, copy.wait_recv)
         rows_all[offset * CAP : (offset + 1) * CAP] = rows_in[order].astype(jnp.float32).reshape(CAP, 8, CX)
 
     for block in range(BLOCKS):
-        total = jnp.zeros((8, CX), jnp.float32)
-        for cross in range(CROSS):
-            source = rows_all[block_index[0, 0, cross, block]].astype(jnp.bfloat16)
-            total += jnp.dot(source, weights[0, 0, block, cross], preferred_element_type=jnp.float32)
+        source = jnp.concatenate(
+            [rows_all[block_index[0, 0, cross, block]] for cross in range(CROSS)], axis=1
+        ).astype(jnp.bfloat16)
+        total = picked(source, weights[0, 0, block].reshape(CROSS * CX, CX))
         blocks_done[block] = total / jnp.maximum(total[6:7], FRAC_FLOOR)
 
     def for_span(span):
@@ -406,7 +431,11 @@
         copy.wait_recv()
     for f in range(6):
         written_ref[0, 0, f] = spans_in[pl.ds(f, n_server, stride=8)]
-    for copy in halo + [copy for _, _, copy in rows_copies] + span_copies:
+    for i, copy in enumerate(halo):
+        where_inside(*SPATIAL[i], copy.wait_send)
+    for _, offset, copy in rows_copies:
+        where_inside(offset - 2, 0, copy.wait_send)
+    for copy in span_copies:
         copy.wait_send()
 
 

time: 38.6 us -> 37 us (0.959)
  the two profiles are of different devices: /device:TPU:1 before, /device:TPU:40 now
where the time goes in v3:
time: 37 us; the launch traced here: 36.9 us
  Pallas kernels  35 us (95%)
  local copies, waits for them, and re-layouts  1.28 us (3%)
  between operations  0.64 us (2%)
    pallas_call x1, Pallas kernels, body(): pl.pallas_call(functools.partial(kernel, n_mp, n_server), out_shape=(pltp...  35 us
    unnamed x2, local copies, waits for them, and re-layouts  1.28 us

profile of v3, /device:TPU:40, one launch (start us, length us, event | category | flops | bytes accessed | tf_op | source)
XLA Modules:
  0.0 36.9 jit_solution(11513993700731018872)
XLA Ops:
  0.6 35.0 %ice.1 = (f32[5,64,128]{2,1,0:T(8,128)S(1)}, f32[1,1,6,8,128]{4,3,2,1,0:T(8,128)S(1)}) custom-call(f32[2,64,128]{2,1,0:T(8,128)} %vel_hbm.1, f32[3,64,128]{2,1,0:T(8,128)} %stress_hbm.1, f32[2,64,128]{2,1,0:T(8,128)} %wind_hbm.1, f32[64,128]{1,0:T(8,128)} %strength_hbm.1, f32[64,128]{1,0:T(8,128)} %mass_hbm.1, s32[64,128]{1,0:T(8,128)} %mask_hbm.1, ...), custom_call_target="tpu_custom_call" | custom-call | tf_op jit(solution)/shard_map/ice/pallas_call | solution.py:463
  35.6 0.7 %copy.14 = f32[5,64,128]{2,1,0:T(8,128)} copy(f32[5,64,128]{2,1,0:T(8,128)S(1)} %get-tuple-element.2) | data formatting | bytes 327680
  36.3 0.6 %copy.15 = f32[1,1,6,8,128]{4,3,2,1,0:T(8,128)} copy(f32[1,1,6,8,128]{4,3,2,1,0:T(8,128)S(1)} %get-tuple-element.3) | data formatting | bytes 49152

commit v4 on v3

--- a/solution.py
+++ b/solution.py
@@ -227,8 +227,6 @@
     def receive_halo(i):
         where_inside(*(-step for step in SPATIAL[i]), lambda: halo[i].wait_recv())
 
-    for i in (2, 3):
-        send_halo(i)
 
     highs = [split(x) for x in own]
     sides = jnp.concatenate(
@@ -249,6 +247,8 @@
     for i in range(4):
         corner_out[i] = corners[CORNER_ROWS * (i // 2) : CORNER_ROWS * (i // 2 + 1), CX * (i % 2) : CX * (i % 2 + 1)]
         send_halo(4 + i)
+    for i in (2, 3):
+        send_halo(i)
 
     for f in range(FIELDS):
         for part in range(2):

time: 37 us -> 36.6 us (0.989)
  the two profiles are of different devices: /device:TPU:40 before, /device:TPU:48 now
where the time goes in v4:
time: 36.6 us; the launch traced here: 36.5 us
  Pallas kernels  34.6 us (95%)
  local copies, waits for them, and re-layouts  1.28 us (3%)
  between operations  0.64 us (2%)
    pallas_call x1, Pallas kernels, body(): pl.pallas_call(functools.partial(kernel, n_mp, n_server), out_shape=(pltp...  34.6 us
    unnamed x2, local copies, waits for them, and re-layouts  1.28 us

profile of v4, /device:TPU:48, one launch (start us, length us, event | category | flops | bytes accessed | tf_op | source)
XLA Modules:
  0.0 36.5 jit_solution(1443434039538579878)
XLA Ops:
  0.6 34.6 %ice.1 = (f32[5,64,128]{2,1,0:T(8,128)S(1)}, f32[1,1,6,8,128]{4,3,2,1,0:T(8,128)S(1)}) custom-call(f32[2,64,128]{2,1,0:T(8,128)} %vel_hbm.1, f32[3,64,128]{2,1,0:T(8,128)} %stress_hbm.1, f32[2,64,128]{2,1,0:T(8,128)} %wind_hbm.1, f32[64,128]{1,0:T(8,128)} %strength_hbm.1, f32[64,128]{1,0:T(8,128)} %mass_hbm.1, s32[64,128]{1,0:T(8,128)} %mask_hbm.1, ...), custom_call_target="tpu_custom_call" | custom-call | tf_op jit(solution)/shard_map/ice/pallas_call | solution.py:463
  35.2 0.7 %copy.14 = f32[5,64,128]{2,1,0:T(8,128)} copy(f32[5,64,128]{2,1,0:T(8,128)S(1)} %get-tuple-element.2) | data formatting | bytes 327680
  35.9 0.6 %copy.15 = f32[1,1,6,8,128]{4,3,2,1,0:T(8,128)} copy(f32[1,1,6,8,128]{4,3,2,1,0:T(8,128)S(1)} %get-tuple-element.3) | data formatting | bytes 49152
